TPU v7x, 768 devices: a whole 4x8x12 slice. The times are simulated.
768 devices in a mesh: grp: 12 (over x, z_hi), col: 64 (over z_lo, y, core).
Axes of the slice: x: 4, y: 8, z: 12 (z_hi: 3, z_lo: 4; z = z_hi * 4 + z_lo), core: 2. Of those that a mesh axis runs over, the one named last changes fastest.
Arguments:
- projected: bfloat16 [64, 1728, 3072], P('col', 'grp'), may hold values from -6 to 6
- out_grad: bfloat16 [64, 1728, 512], P('col', 'grp'), may hold values from -6 to 6
- w_out: bfloat16 [768, 512], replicated, may hold values from -0.21875 to 0.21875
- owners: int32 [64, 144], P('col', 'grp'), may hold values from 0 to 11, as said below
- slots: int32 [64, 144], P('col', 'grp'), may hold values from 0 to 11, as said below
- lengths: int32 [64, 144], P('col', 'grp'), may hold values from 0 to 144, as said below
Outputs:
- branch_out: bfloat16 [64, 1728, 512], P('col', 'grp')
- projected_grad: bfloat16 [64, 1728, 3072], P('col', 'grp')
- output_weight_grad: float32 [768, 512], P('grp', 'col')
Inputs may be any that keep to these rules, and one draw needn't show every extreme that they name: In every group, the 12 blocks of each grp index have 12 different owners. In every group, the blocks sent to one owner take each of its 12 slots once. `lengths`: in every group, slot 0 of each owner starts a history; a history that covers k slots has a length over 12 * (k - 1) and at most 12 * k; in every group one owner holds a single history of 144 rows.
All inputs are finite; a program needn't handle non-finite values.
Results may differ from a plain program's by a relative error of at most 0.0063.
Values may be sent and summed in bfloat16 or wider, within the bound.
A program may use at most 128 MiB of HBM per device.

v0:
```python
import math

import jax
import jax.numpy as jnp
from jax import lax
from jax.sharding import PartitionSpec as P

DH = 128


def history_layout(starts, block_rows):
    count = starts.shape[0]
    opened = (starts > 0).astype(jnp.int32)
    segment = jnp.cumsum(opened) - 1
    places = jnp.arange(count, dtype=jnp.int32)
    shared = segment[:, None] == segment[None, :]
    first = jnp.min(jnp.where(shared, places[None, :], count), axis=1)
    length = jnp.sum(jnp.where(places[None, :] == first[:, None], starts[None, :], 0), axis=1)
    inner = jnp.arange(count * block_rows, dtype=jnp.int32)
    block_of = inner // block_rows
    row_segment = jnp.repeat(segment, block_rows)
    position = (block_of - jnp.repeat(first, block_rows)) * block_rows + inner % block_rows
    row_length = jnp.repeat(length, block_rows)
    valid = position < row_length
    mask = (
        (row_segment[:, None] == row_segment[None, :])
        & (inner[None, :] <= inner[:, None])
        & valid[:, None]
    )
    return (mask, valid, row_length)


def score_product(form, left, right):
    return jnp.einsum(form, left, right, preferred_element_type=jnp.float32)


def owner_step(stacked, branch, starts, block_rows):
    mask, valid, row_length = history_layout(starts, block_rows)
    row_counts_total, width = stacked.shape
    feature_rows = width // 4
    heads = feature_rows // DH
    gate = stacked[:, :feature_rows].astype(jnp.float32)
    value_rows = stacked[:, feature_rows : 2 * feature_rows].reshape(row_counts_total, heads, DH)
    query_rows = stacked[:, 2 * feature_rows : 3 * feature_rows].reshape(
        row_counts_total, heads, DH
    )
    key_rows = stacked[:, 3 * feature_rows :].reshape(row_counts_total, heads, DH)
    score_scale = 1.0 / math.sqrt(DH)
    score_matrix = score_product("uej,kej->euk", query_rows, key_rows) * score_scale
    inverse = (1.0 / row_length.astype(jnp.float32))[None, :, None]
    weights = jnp.where(mask[None], jax.nn.silu(score_matrix), 0.0) * inverse
    weights_reduced_precision = weights.astype(jnp.bfloat16)
    attended_output = score_product("xry,yxk->rxk", weights_reduced_precision, value_rows).reshape(
        row_counts_total, feature_rows
    )
    centre = jnp.mean(attended_output, axis=-1, keepdims=True)
    spread = jnp.mean((attended_output - centre) ** 2, axis=-1, keepdims=True)
    rstd = lax.rsqrt(spread + 1e-05)
    normed = (attended_output - centre) * rstd
    mixed = (normed * gate).astype(jnp.bfloat16)
    upstream = branch.astype(jnp.float32)
    gate_grad = (upstream * normed).astype(jnp.bfloat16)
    normed_grad = upstream * gate
    attended_output_grad = rstd * (
        normed_grad
        - jnp.mean(normed_grad, axis=-1, keepdims=True)
        - normed * jnp.mean(normed_grad * normed, axis=-1, keepdims=True)
    )
    attended_output_grad = (
        jnp.where(valid[:, None], attended_output_grad, 0.0)
        .astype(jnp.bfloat16)
        .reshape(row_counts_total, heads, DH)
    )
    output_weight_grad = score_product("uej,kej->euk", attended_output_grad, value_rows)
    value_rows_grad = score_product(
        "ove,vox->eox", weights_reduced_precision, attended_output_grad
    ).astype(jnp.bfloat16)
    sigma = jax.nn.sigmoid(score_matrix)
    scores_gradient = (
        jnp.where(
            mask[None], output_weight_grad * sigma * (1.0 + score_matrix * (1.0 - sigma)), 0.0
        )
        * inverse
    ).astype(jnp.bfloat16)
    query_rows_grad = (
        score_product("xry,yxk->rxk", scores_gradient, key_rows) * score_scale
    ).astype(jnp.bfloat16)
    key_rows_grad = (
        score_product("ove,vox->eox", scores_gradient, query_rows) * score_scale
    ).astype(jnp.bfloat16)
    grads = jnp.concatenate(
        [
            gate_grad,
            value_rows_grad.reshape(row_counts_total, feature_rows),
            query_rows_grad.reshape(row_counts_total, feature_rows),
            key_rows_grad.reshape(row_counts_total, feature_rows),
        ],
        axis=-1,
    )
    return (grads, mixed)


def transposed_product(left, right):
    return lax.dot_general(
        left, right, (((0,), (0,)), ((), ())), preferred_element_type=jnp.float32
    )


def per_device(projected, out_grad, w_out, owners, slots, lengths):
    rows, width = (projected.shape[1], projected.shape[2])
    count = owners.shape[1]
    block_rows = rows // count
    feature_rows, model_width = w_out.shape
    stacked = projected[0]
    upstream = out_grad[0]
    owner_of = owners[0]
    slot_of = slots[0]
    starts = lengths[0]
    sorting = jnp.argsort(owner_of)
    send_slots = slot_of[sorting]
    sent = stacked.reshape(count, block_rows, width)[sorting]
    branch = lax.dot_general(
        upstream, w_out, (((1,), (1,)), ((), ())), preferred_element_type=jnp.float32
    ).astype(jnp.bfloat16)
    arrived, arrived_branch, arrived_slots = (
        lax.all_to_all(sent, "grp", split_axis=0, concat_axis=0, tiled=True),
        lax.all_to_all(
            branch.reshape(count, block_rows, feature_rows)[sorting],
            "grp",
            split_axis=0,
            concat_axis=0,
            tiled=True,
        ),
        lax.all_to_all(send_slots, "grp", split_axis=0, concat_axis=0, tiled=True),
    )
    placing = jnp.argsort(arrived_slots)
    grads, mixed = owner_step(
        arrived[placing].reshape(rows, width),
        arrived_branch[placing].reshape(rows, feature_rows),
        starts,
        block_rows,
    )
    back_grads, back_mixed = (
        lax.all_to_all(
            grads.reshape(count, block_rows, width)[arrived_slots],
            "grp",
            split_axis=0,
            concat_axis=0,
            tiled=True,
        ),
        lax.all_to_all(
            mixed.reshape(count, block_rows, feature_rows)[arrived_slots],
            "grp",
            split_axis=0,
            concat_axis=0,
            tiled=True,
        ),
    )
    grads_home = back_grads[owner_of].reshape(rows, width)
    mixed_rows = back_mixed[owner_of].reshape(rows, feature_rows)
    output = jnp.dot(mixed_rows, w_out, preferred_element_type=jnp.float32).astype(jnp.bfloat16)
    partial_rows = lax.psum_scatter(
        transposed_product(mixed_rows, upstream), "grp", scatter_dimension=0, tiled=True
    )
    weight_part = lax.psum_scatter(partial_rows, "col", scatter_dimension=1, tiled=True)
    return (output[None], grads_home[None], weight_part)


def solution(mesh):
    return jax.shard_map(
        per_device,
        mesh=mesh,
        in_specs=(
            P("col", "grp", None),
            P("col", "grp", None),
            P(),
            P("col", "grp"),
            P("col", "grp"),
            P("col", "grp"),
        ),
        out_specs=(P("col", "grp", None), P("col", "grp", None), P("grp", "col")),
        check_vma=False,
    )
```

profile of v0, /device:TPU:1, one launch (start us, length us, event | category | flops | bytes accessed | tf_op | source)
XLA Modules:
  0.0 801.8 jit_solution(17087363846904944412)
XLA Ops:
  7.2 2.0 sort.31
  9.2 1.3 gather_fusion.1
  10.5 0.7 copy.62
  11.2 17.0 %all-to-all-start.1 = ((s32[12,1,1]{2,1,0:T(1,128)}), s32[12,1,1]{2,1,0:T(1,128)S(1)}, u32[]{:S(2)}, u32[]{:S(2)}) async-start(s32[12,1,1]{2,1,0:T(1,128)} %copy.62), calls=%async_computation.1 | async-start | bytes 12288 | tf_op jit(solution)/shard_map/all_to_all | solution.py:134
  28.2 1.4 convolution_convert_fusion.1
  29.6 1.3 gather_fusion.5
  30.9 6.1 all-to-all-done.1
  37.0 4.6 all-to-all-start.3
  41.8 1.7 gather_fusion
  43.5 10.0 %all-to-all-done.3 = bf16[12,12,768]{2,1,0:T(8,128)(2,1)S(1)} async-done(((bf16[12,12,768]{2,1,0:T(8,128)(2,1)}), bf16[12,12,768]{2,1,0:T(8,128)(2,1)S(1)}, u32[]{:S(2)}, u32[]{:S(2)}) %all-to-all-start.3) | async-done | bytes 221216 | tf_op jit(solution)/shard_map/all_to_all | solution.py:127
  53.5 6.9 all-to-all-start
  61.6 0.3 reduce.3
  61.9 1.3 sort.32
  63.2 0.6 gather_fusion.6
  63.8 0.8 reshape.303
  64.6 42.2 %all-to-all-done = bf16[12,12,3072]{2,1,0:T(8,128)(2,1)S(1)} async-done(((bf16[12,12,3072]{2,1,0:T(8,128)(2,1)}), bf16[12,12,3072]{2,1,0:T(8,128)(2,1)S(1)}, u32[]{:S(2)}, u32[]{:S(2)}) %all-to-all-start) | async-done | bytes 884768 | tf_op jit(solution)/shard_map/all_to_all | solution.py:126
  106.8 0.6 gather_fusion.2
  107.7 1.4 multiply_convert_fusion
  109.2 0.4 fusion.45
  109.5 0.2 multiply_reduce_fusion.1
  109.8 0.4 copy-done.3
  110.2 0.3 copy-done.2
  110.5 0.2 fusion.35
  110.7 0.3 fusion.12
  111.0 1.3 gather_fusion.3
  112.3 3.5 all-to-all-start.2
  115.9 2.4 fusion.3
  118.4 1.4 fusion.7
  119.8 8.2 %all-to-all-done.2 = bf16[12,12,768]{2,1,0:T(8,128)(2,1)S(1)} async-done(((bf16[12,12,768]{2,1,0:T(8,128)(2,1)}), bf16[12,12,768]{2,1,0:T(8,128)(2,1)S(1)}, u32[]{:S(2)}, u32[]{:S(2)}) %all-to-all-start.2) | async-done | bytes 221216 | tf_op jit(solution)/shard_map/all_to_all | solution.py:151
  127.9 0.6 gather_fusion.4
  128.6 1.6 fusion.30
  130.2 0.9 copy-done.9
  131.1 1.3 fusion.6
  132.6 0.3 concatenate.12
  133.0 1.0 concatenate.11
  134.0 0.4 fusion.8
  134.4 1.0 concatenate.10
  135.9 0.7 copy-done.4
  136.8 1.7 gather_fusion.7
  138.5 3.7 all-to-all-start.4
  142.2 1.3 dynamic-slice
  144.2 171.5 %reduce-scatter.3.cloned.1.call-done = f32[64,512]{1,0:T(8,128)} async-done(((f32[768,512]{1,0:T(8,128)}), f32[64,512]{1,0:T(8,128)}) %reduce-scatter.3.cloned.1.call-update) | async-done | bytes 131088 | tf_op jit(solution)/shard_map/reduce_scatter | solution.py:162
  315.7 1.0 fusion.9
  316.6 0.6 gather_fusion.8
  317.3 1.1 broadcast_in_dim_reshape.2
  318.4 475.1 %all-reduce.3.cloned.1.call-done = f32[64,512]{1,0:T(8,128)} async-done(((f32[64,512]{1,0:T(8,128)}), f32[64,512]{1,0:T(8,128)}) %all-reduce.3.cloned.1.call-update) | async-done | bytes 131088
  793.4 0.8 constant_dynamic-slice_fusion
  794.3 0.7 copy.78
  (67 shorter events, 3.1 us)
Async XLA Ops:
  7.2 21.0 %copy-start = (bf16[768,512]{1,0:T(8,128)(2,1)S(1)}, bf16[768,512]{1,0:T(8,128)(2,1)}, u32[]{:S(2)}) copy-start(bf16[768,512]{1,0:T(8,128)(2,1)} %param.8) | copy-start | bytes 2359300
  11.2 25.8 %all-to-all-start.1 = ((s32[12,1,1]{2,1,0:T(1,128)}), s32[12,1,1]{2,1,0:T(1,128)S(1)}, u32[]{:S(2)}, u32[]{:S(2)}) async-start(s32[12,1,1]{2,1,0:T(1,128)} %copy.62), calls=%async_computation.1 | async-start | bytes 12288 | tf_op jit(solution)/shard_map/all_to_all | solution.py:134
  28.2 13.4 %copy-start.6 = (bf16[1,144,3072]{2,1,0:T(8,128)(2,1)S(1)}, bf16[1,144,3072]{2,1,0:T(8,128)(2,1)}, u32[]{:S(2)}) copy-start(bf16[1,144,3072]{2,1,0:T(8,128)(2,1)} %param.6) | copy-start | bytes 2654212
  37.0 16.5 %all-to-all-start.3 = ((bf16[12,12,768]{2,1,0:T(8,128)(2,1)}), bf16[12,12,768]{2,1,0:T(8,128)(2,1)S(1)}, u32[]{:S(2)}, u32[]{:S(2)}) async-start(bf16[12,12,768]{2,1,0:T(8,128)(2,1)} %gather_fusion.5), calls=%async_computation.3 | async-start | bytes 589824 | tf_op jit(solution)/shard_map/all_to_all | solution.py:127
  43.5 16.9 %copy-start.10 = (s32[1,12]{1,0:T(1,128)S(1)}, s32[1,12]{1,0:T(1,128)}, u32[]{:S(2)}) copy-start(s32[1,12]{1,0:T(1,128)} %param.11) | copy-start | bytes 148
  43.5 18.0 %copy-start.11 = (s32[1,12]{1,0:T(1,128)S(1)}, s32[1,12]{1,0:T(1,128)}, u32[]{:S(2)}) copy-start(s32[1,12]{1,0:T(1,128)} %param.9) | copy-start | bytes 148
  53.5 53.3 %all-to-all-start = ((bf16[12,12,3072]{2,1,0:T(8,128)(2,1)}), bf16[12,12,3072]{2,1,0:T(8,128)(2,1)S(1)}, u32[]{:S(2)}, u32[]{:S(2)}) async-start(bf16[12,12,3072]{2,1,0:T(8,128)(2,1)} %gather_fusion), calls=%async_computation | async-start | bytes 2359296 | tf_op jit(solution)/shard_map/all_to_all | solution.py:126
  107.7 1.5 copy-start.1
  107.7 1.4 copy-start.8
  109.2 1.0 copy-start.3
  109.2 1.3 copy-start.2
  112.3 15.6 %all-to-all-start.2 = ((bf16[12,12,768]{2,1,0:T(8,128)(2,1)}), bf16[12,12,768]{2,1,0:T(8,128)(2,1)S(1)}, u32[]{:S(2)}, u32[]{:S(2)}) async-start(bf16[12,12,768]{2,1,0:T(8,128)(2,1)} %gather_fusion.3), calls=%async_computation.2 | async-start | bytes 589824 | tf_op jit(solution)/shard_map/all_to_all | solution.py:151
  115.9 199.8 %reduce-scatter.3.cloned.1.call-start = ((), (), s32[]{:S(2)}) async-start(), calls=%async_computation.6 | async-start | bytes 1703936 | tf_op jit(solution)/shard_map/reduce_scatter | solution.py:162
  119.8 8.8 %copy-start.7 = (bf16[1,144,512]{2,1,0:T(8,128)(2,1)S(1)}, bf16[1,144,512]{2,1,0:T(8,128)(2,1)}, u32[]{:S(2)}) copy-start(bf16[1,144,512]{2,1,0:T(8,128)(2,1)} %param.7) | copy-start | bytes 442372
  130.2 0.9 copy-start.9
  135.5 1.0 copy-start.4
  135.7 1.0 copy-start.5
  138.5 178.2 %all-to-all-start.4 = ((bf16[12,12,3072]{2,1,0:T(8,128)(2,1)}), bf16[12,12,3072]{2,1,0:T(8,128)(2,1)S(1)}, u32[]{:S(2)}, u32[]{:S(2)}) async-start(bf16[12,12,3072]{2,1,0:T(8,128)(2,1)} %gather_fusion.7), calls=%async_computation.4 | async-start | bytes 2359296 | tf_op jit(solution)/shard_map/all_to_all | solution.py:144
  142.2 651.3 %all-reduce.3.cloned.1.call-start = ((), (), s32[]{:S(2)}) async-start(), calls=%async_computation.7 | async-start | bytes 262144
Sparse Core Ops, SparseCore 0:
  130.3 185.3 reduce-scatter.2
  318.9 474.5 all-reduce.2
where the time goes:
time: 803 us; the launch traced here: 802 us
  waiting for transfers between devices  713 us (89%)
  starting transfers between devices  35.8 us (4%)
  local copies, waits for them, and re-layouts  21.4 us (3%)
  between operations  15.1 us (2%)
  matrix products  11.1 us (1%)
    unnamed x3, waiting for transfers between devices  475 us
    reduce_scatter x1, waiting for transfers between devices, per_device(): lax.psum_scatter(transposed_product(mixed_rows, upstream), 'grp', scatter...  171 us
    all_to_all x1, waiting for transfers between devices, per_device(): lax.all_to_all(sent, 'grp', split_axis=0, concat_axis=0, tiled=True)  42.2 us
    all_to_all x1, starting transfers between devices, per_device(): lax.all_to_all(send_slots, 'grp', split_axis=0, concat_axis=0, tiled=True)  17 us
  transfers between devices with their start and end apart: 7, of which 6 were waited for; matrix products, arithmetic and copies ran while one was open for 3% of the time, Pallas kernels for 0%

commit v1 on v0

v1 whole, which is shorter than its diff:
```python
import functools
import math

import jax
import jax.numpy as jnp
from jax import lax
from jax.experimental import pallas as pl
from jax.experimental.pallas import tpu as pltpu
from jax.sharding import PartitionSpec as P

DH = 128
HEADS = 6
HD = 768
BR = 12
PR = 16
NG = 12
NZ, NY, NC = 4, 8, 2
ROWS = BR * NG
PROWS = PR * NG
MESH = pl.DeviceIdType.MESH
BF = jnp.bfloat16
F32 = jnp.float32


def mm(a, b):
    return lax.dot_general(a, b, (((1,), (0,)), ((), ())), preferred_element_type=F32)


def mm_nt(a, b):
    return lax.dot_general(a, b, (((1,), (1,)), ((), ())), preferred_element_type=F32)


def mm_tn(a, b):
    return lax.dot_general(a, b, (((0,), (0,)), ((), ())), preferred_element_type=F32)


def onehot(cond):
    return jnp.where(cond, 1.0, 0.0).astype(BF)


def iota(shape, dim):
    return lax.broadcasted_iota(jnp.int32, shape, dim)


def fold_in(mats, natural, pair):
    parts = [mm(mats[b], pair) for b in range(3)]
    extra = jnp.concatenate([p[:, :DH] for p in parts] + [p[:, DH:] for p in parts], axis=1)
    return (natural + extra).astype(BF)


def fold_out(mats, chunk):
    total = None
    for b in range(3):
        pair = jnp.concatenate(
            [chunk[:, b * DH : (b + 1) * DH], chunk[:, (3 + b) * DH : (4 + b) * DH]], axis=1
        )
        term = mm(mats[b], pair)
        total = term if total is None else total + term
    return total


def head(h):
    return slice(h * DH, (h + 1) * DH)


def kernel(
    own_s, slot_s, len_s, x_ref, og_ref, w_ref,
    bo_ref, pg_ref, dw_ref,
    cs, cr, rs, rr, ts, tr, p_scr, f_scr, dwf, d1s, d1r, d2s, d2r, d3s, d3r, d4s, d4r,
    c_ssem, c_rsem, r_ssem, r_rsem, t_ssem, t_rsem,
    d1_ssem, d1_rsem, d2_ssem, d2_rsem, d3_ssem, d3_rsem, d4_ssem, d4_rsem,
):
    g = lax.axis_index("grp")
    col = lax.axis_index("col")
    core = lax.rem(col, NC)
    y = lax.rem(col // NC, NY)
    zl = col // (NC * NY)

    def col_of(z_, y_, c_):
        return (z_ * NY + y_) * NC + c_

    other = col_of(zl, y, 1 - core)

    barrier = pltpu.get_barrier_semaphore()

    def greet(k, c):
        pl.semaphore_signal(
            barrier, inc=1, device_id=(lax.rem(g + k, NG), col), device_id_type=MESH
        )
        return c

    lax.fori_loop(1, NG, greet, 0)
    pl.semaphore_signal(barrier, inc=1, device_id=(g, other), device_id_type=MESH)

    def greet_y(k, c):
        pl.semaphore_signal(
            barrier, inc=1, device_id=(g, col_of(zl, lax.rem(y + k, NY), core)), device_id_type=MESH
        )
        return c

    lax.fori_loop(1, NY, greet_y, 0)

    def greet_z(k, c):
        pl.semaphore_signal(
            barrier, inc=1, device_id=(g, col_of(lax.rem(zl + k, NZ), y, core)), device_id_type=MESH
        )
        return c

    lax.fori_loop(1, NZ, greet_z, 0)

    def grp_copy(src, dst, ssem, rsem, k):
        peer = lax.rem(g + k, NG)
        return pltpu.make_async_remote_copy(
            src_ref=src.at[peer], dst_ref=dst.at[g], send_sem=ssem.at[peer], recv_sem=rsem.at[g],
            device_id=(peer, col), device_id_type=MESH,
        )

    def grp_start(src, dst, ssem, rsem):
        def body(k, c):
            grp_copy(src, dst, ssem, rsem, k).start()
            return c

        lax.fori_loop(1, NG, body, 0)

    def grp_wait_recv(src, dst, ssem, rsem):
        def body(k, c):
            peer = lax.rem(g + k, NG)
            pltpu.make_async_remote_copy(
                src_ref=src.at[peer], dst_ref=dst.at[peer], send_sem=ssem.at[peer],
                recv_sem=rsem.at[peer], device_id=(peer, col), device_id_type=MESH,
            ).wait_recv()
            return c

        lax.fori_loop(1, NG, body, 0)

    def grp_wait_send(src, dst, ssem, rsem):
        def body(k, c):
            grp_copy(src, dst, ssem, rsem, k).wait_send()
            return c

        lax.fori_loop(1, NG, body, 0)

    lane = iota((8, ROWS), 1)
    own_c = jnp.zeros((8, ROWS), jnp.int32)
    in_c = lane
    for j in range(NG):
        own_c = jnp.where(lane >= BR * j, own_s[0, j], own_c)
        in_c = jnp.where(lane >= BR * j, lane - BR * j, in_c)
    own_c, in_c = own_c[:1], in_c[:1]
    rows = iota((PROWS, ROWS), 0)
    same = (rows >> 4) == own_c
    in_r = rows & 15
    send_nat = onehot(same & (in_r == in_c))
    send_fold = [onehot(same & (in_r - BR + 4 * b == in_c) & (in_r >= BR)) for b in range(3)]

    def put(i, chunk):
        cs[i] = chunk.reshape(NG, PR, HD)
        cr[i, g] = cs[i, g]

    q = x_ref[:, 2 * HD : 3 * HD]
    put(0, fold_in(send_fold, mm(send_nat, q), x_ref[:, 3 * HD : 3 * HD + 2 * DH]))
    for o in range(NG):
        tile = jnp.zeros((PR, DH), jnp.int32)
        for j in range(NG):
            tile = jnp.where(jnp.full((PR, DH), own_s[0, j]) == o, slot_s[0, j], tile)
        ts[o] = tile.astype(F32)
    tr[g] = ts[g]

    pl.semaphore_wait(barrier, NG - 1 + 1 + NY - 1 + NZ - 1)

    grp_start(ts, tr, t_ssem, t_rsem)
    grp_start(cs.at[0], cr.at[0], c_ssem.at[0], c_rsem.at[0])
    nat = jnp.concatenate([x_ref[:, 3 * HD + 2 * DH : 4 * HD], x_ref[:, HD : HD + 2 * DH]], axis=1)
    put(1, fold_in(send_fold, mm(send_nat, nat), x_ref[:, HD + 2 * DH : HD + 4 * DH]))
    grp_start(cs.at[1], cr.at[1], c_ssem.at[1], c_rsem.at[1])
    branch = mm_nt(og_ref[...], w_ref[...]).astype(BF).astype(F32)
    gate = x_ref[:, :HD].astype(F32)
    grad = (branch * gate).astype(BF)
    put(2, fold_in(send_fold, mm(send_nat, grad), x_ref[:, HD + 4 * DH : 2 * HD]))
    grp_start(cs.at[2], cr.at[2], c_ssem.at[2], c_rsem.at[2])

    rows = iota((PROWS, PROWS), 0)
    cols = iota((PROWS, PROWS), 1)
    same = (rows >> 4) == (cols >> 4)
    rr_, cc_ = rows & 15, cols & 15
    unfold = [onehot(same & (cc_ >= BR) & (rr_ == cc_ - BR + 4 * b)) for b in range(3)]
    infold = [onehot(same & (rr_ >= BR) & (cc_ == rr_ - BR + 4 * b)) for b in range(3)]

    rows = iota((ROWS, PROWS), 0)
    cols = iota((ROWS, PROWS), 1)
    own_r = jnp.zeros((ROWS, PROWS), jnp.int32)
    in_b = rows
    for j in range(NG):
        own_r = jnp.where(rows >= BR * j, own_s[0, j], own_r)
        in_b = jnp.where(rows >= BR * j, rows - BR * j, in_b)
    same = own_r == (cols >> 4)
    cc_ = cols & 15
    home_nat = onehot(same & (cc_ == in_b))
    home_fold = [onehot(same & (cc_ >= BR) & (cc_ - BR + 4 * b == in_b)) for b in range(3)]

    grp_wait_recv(ts, tr, t_ssem, t_rsem)
    slot_r = tr[...].reshape(PROWS, DH)
    lane = iota((8, PROWS), 1)
    slot_c = jnp.zeros((8, PROWS), F32)
    for d in range(NG):
        slot_c = jnp.where((lane >> 4) == d, tr[d, :8, :1], slot_c)
    first = jnp.int32(0)
    length = jnp.int32(1)
    first_r, len_r = jnp.zeros((PROWS, DH), F32), jnp.ones((PROWS, DH), F32)
    first_c = jnp.zeros((8, PROWS), F32)
    for s in range(NG):
        start = len_s[0, s]
        opened = start > 0
        first = jnp.where(opened, s, first)
        length = jnp.where(opened, start, length)
        first_f, length_f = first.astype(F32), length.astype(F32)
        first_r = jnp.where(slot_r == float(s), first_f, first_r)
        len_r = jnp.where(slot_r == float(s), length_f, len_r)
        first_c = jnp.where(slot_c == float(s), first_f, first_c)
    sub = iota((PROWS, DH), 0) & 15
    pos_r = (slot_r - first_r) * BR + sub.astype(F32)
    valid_r = (pos_r < len_r) & (sub < BR)
    pos_c = (slot_c - first_c) * BR + (lane & 15).astype(F32)
    pos_c = jnp.where((lane & 15) < BR, pos_c, 1e9)
    inv_r = jnp.where(valid_r, 1.0 / len_r, 0.0)
    valid = jnp.where(valid_r, 1.0, 0.0)[:, :1]
    weight = jnp.where(
        (first_r[:, :1] == first_c[:1]) & (pos_c[:1] <= pos_r[:, :1]), inv_r[:, :1], 0.0
    )

    scale = 1.0 / math.sqrt(DH)

    def chunk_in(i):
        grp_wait_recv(cs.at[i], cr.at[i], c_ssem.at[i], c_rsem.at[i])
        return cr[i].reshape(PROWS, HD)

    c0 = chunk_in(0)
    k01 = fold_out(unfold, c0).astype(BF)
    qs = [c0[:, head(h)] for h in range(HEADS)]

    def scores(h, kh):
        s = mm_nt(qs[h], kh) * scale
        sig = jax.nn.sigmoid(s)
        p_scr[h] = (s * sig * weight).astype(BF)
        f_scr[h] = sig * (1.0 + s * (1.0 - sig)) * weight

    scores(0, k01[:, :DH])
    scores(1, k01[:, DH:])
    c1 = chunk_in(1)
    ks = [k01[:, :DH], k01[:, DH:]] + [c1[:, head(h)] for h in range(4)]
    for h in range(2, HEADS):
        scores(h, ks[h])
    v23 = fold_out(unfold, c1).astype(BF)
    vs = [c1[:, head(4)], c1[:, head(5)], v23[:, :DH], v23[:, DH:]]
    attended = [mm(p_scr[h], vs[h]) for h in range(4)]
    c2 = chunk_in(2)
    v45 = fold_out(unfold, c2).astype(BF)
    vs += [v45[:, :DH], v45[:, DH:]]
    attended += [mm(p_scr[h], vs[h]) for h in range(4, HEADS)]
    att = jnp.concatenate(attended, axis=1)
    centre = jnp.mean(att, axis=1, keepdims=True)
    att = att - centre
    rstd = lax.rsqrt(jnp.mean(att * att, axis=1, keepdims=True) + 1e-05)
    normed = att * rstd

    gr = c2.astype(F32)
    datt = rstd * (
        gr - jnp.mean(gr, axis=1, keepdims=True)
        - normed * jnp.mean(gr * normed, axis=1, keepdims=True)
    )
    datt = jnp.where(valid > 0.5, datt, 0.0).astype(BF)

    def back(i, natural, pair):
        rs[i] = fold_in(infold, natural, pair.astype(BF)).reshape(NG, PR, HD)
        rr[i, g] = rs[i, g]
        grp_start(rs.at[i], rr.at[i], r_ssem.at[i], r_rsem.at[i])

    def dv(h):
        return mm_tn(p_scr[h], datt[:, head(h)])

    back(0, normed, jnp.concatenate([dv(0), dv(1)], axis=1))

    def dqk(h):
        ds = (mm_nt(datt[:, head(h)], vs[h]) * f_scr[h]).astype(BF)
        return [mm(ds, ks[h]) * scale, mm_tn(ds, qs[h]) * scale]

    back(1, jnp.concatenate(dqk(0) + dqk(1) + dqk(2), axis=1), jnp.concatenate([dv(2), dv(3)], axis=1))
    back(2, jnp.concatenate(dqk(3) + dqk(4) + dqk(5), axis=1), jnp.concatenate([dv(4), dv(5)], axis=1))

    def chunk_home(i):
        grp_wait_recv(rs.at[i], rr.at[i], r_ssem.at[i], r_rsem.at[i])
        chunk = rr[i].reshape(PROWS, HD)
        return mm(home_nat, chunk), chunk

    n_home, chunk = chunk_home(0)
    branch = mm_nt(og_ref[...], w_ref[...]).astype(BF).astype(F32)
    z = (n_home * gate).astype(BF)

    dwf[...] = mm_tn(og_ref[...], z).reshape(NZ, NY, NC, 8, HD)
    for yy in range(NY):
        d1s[yy] = jnp.concatenate([dwf[zz, yy, 1 - core] for zz in range(NZ)], axis=0).astype(BF)
    d1 = pltpu.make_async_remote_copy(
        src_ref=d1s, dst_ref=d1r, send_sem=d1_ssem, recv_sem=d1_rsem,
        device_id=(g, other), device_id_type=MESH,
    )
    d1.start()
    pg_ref[:, :HD] = (branch * n_home).astype(BF)
    pg_ref[:, HD : HD + 2 * DH] = fold_out(home_fold, chunk).astype(BF)
    bo_ref[...] = mm(z, w_ref[...]).astype(BF)
    d1.wait_recv()
    for yy in range(NY):
        mine = jnp.concatenate([dwf[zz, yy, core] for zz in range(NZ)], axis=0)
        d2s[yy] = (mine + d1r[yy].astype(F32)).astype(BF)

    def d2(k, slot):
        peer = lax.rem(y + k, NY)
        return pltpu.make_async_remote_copy(
            src_ref=d2s.at[peer], dst_ref=d2r.at[peer if slot else y], send_sem=d2_ssem.at[peer],
            recv_sem=d2_rsem.at[peer if slot else y],
            device_id=(g, col_of(zl, peer, core)), device_id_type=MESH,
        )

    def d2_start(k, c):
        d2(k, False).start()
        return c

    lax.fori_loop(1, NY, d2_start, 0)
    d2r[y] = d2s[y]

    back1, chunk = chunk_home(1)
    back1 = back1.astype(BF)
    for h in range(3):
        pg_ref[:, 2 * HD + h * DH : 2 * HD + (h + 1) * DH] = back1[:, head(2 * h)]
        pg_ref[:, 3 * HD + h * DH : 3 * HD + (h + 1) * DH] = back1[:, head(2 * h + 1)]
    pg_ref[:, HD + 2 * DH : HD + 4 * DH] = fold_out(home_fold, chunk).astype(BF)

    def d2_wait(k, c):
        d2(k, True).wait_recv()
        return c

    lax.fori_loop(1, NY, d2_wait, 0)
    total = d2r[0].astype(F32)
    for yy in range(1, NY):
        total = total + d2r[yy].astype(F32)
    d3s[...] = total.reshape(NZ, 8, HD)

    def d3(k, slot):
        peer = lax.rem(zl + k, NZ)
        return pltpu.make_async_remote_copy(
            src_ref=d3s.at[peer], dst_ref=d3r.at[peer if slot else zl], send_sem=d3_ssem.at[peer],
            recv_sem=d3_rsem.at[peer if slot else zl],
            device_id=(g, col_of(peer, y, core)), device_id_type=MESH,
        )

    def d3_start(k, c):
        d3(k, False).start()
        return c

    lax.fori_loop(1, NZ, d3_start, 0)
    d3r[zl] = d3s[zl]

    def d3_wait(k, c):
        d3(k, True).wait_recv()
        return c

    lax.fori_loop(1, NZ, d3_wait, 0)
    total = d3r[0] + d3r[1] + d3r[2] + d3r[3]
    for o in range(NG):
        d4s[o, :, :64] = total[:, 64 * o : 64 * o + 64]
        d4s[o, :, 64:] = jnp.zeros((8, 64), F32)
    grp_start(d4s, d4r, d4_ssem, d4_rsem)
    d4r[g] = d4s[g]

    back2, chunk = chunk_home(2)
    back2 = back2.astype(BF)
    for h in range(3):
        pg_ref[:, 2 * HD + (h + 3) * DH : 2 * HD + (h + 4) * DH] = back2[:, head(2 * h)]
        pg_ref[:, 3 * HD + (h + 3) * DH : 3 * HD + (h + 4) * DH] = back2[:, head(2 * h + 1)]
    pg_ref[:, HD + 4 * DH : 2 * HD] = fold_out(home_fold, chunk).astype(BF)

    grp_wait_recv(d4s, d4r, d4_ssem, d4_rsem)
    total = d4r[0]
    for o in range(1, NG):
        total = total + d4r[o]
    dw_ref[...] = jnp.transpose(total)[:64, :]

    grp_wait_send(ts, tr, t_ssem, t_rsem)
    for i in range(3):
        grp_wait_send(cs.at[i], cr.at[i], c_ssem.at[i], c_rsem.at[i])
        grp_wait_send(rs.at[i], rr.at[i], r_ssem.at[i], r_rsem.at[i])
    d1.wait_send()

    def d2_sent(k, c):
        d2(k, False).wait_send()
        return c

    lax.fori_loop(1, NY, d2_sent, 0)

    def d3_sent(k, c):
        d3(k, False).wait_send()
        return c

    lax.fori_loop(1, NZ, d3_sent, 0)
    grp_wait_send(d4s, d4r, d4_ssem, d4_rsem)


def per_device(projected, out_grad, w_out, owners, slots, lengths):
    dma = pltpu.SemaphoreType.DMA
    vmem = pl.BlockSpec(memory_space=pltpu.VMEM)
    smem = pl.BlockSpec(memory_space=pltpu.SMEM)
    bo, pg, dw = pl.pallas_call(
        kernel,
        out_shape=(
            jax.ShapeDtypeStruct((ROWS, 512), BF),
            jax.ShapeDtypeStruct((ROWS, 4 * HD), BF),
            jax.ShapeDtypeStruct((64, 8), F32),
        ),
        in_specs=[smem, smem, smem, vmem, vmem, vmem],
        out_specs=(vmem, vmem, vmem),
        scratch_shapes=[
            pltpu.VMEM((3, NG, PR, HD), BF),
            pltpu.VMEM((3, NG, PR, HD), BF),
            pltpu.VMEM((3, NG, PR, HD), BF),
            pltpu.VMEM((3, NG, PR, HD), BF),
            pltpu.VMEM((NG, PR, DH), F32),
            pltpu.VMEM((NG, PR, DH), F32),
            pltpu.VMEM((HEADS, PROWS, PROWS), BF),
            pltpu.VMEM((HEADS, PROWS, PROWS), F32),
            pltpu.VMEM((NZ, NY, NC, 8, HD), F32),
            pltpu.VMEM((NY, 32, HD), BF),
            pltpu.VMEM((NY, 32, HD), BF),
            pltpu.VMEM((NY, 32, HD), BF),
            pltpu.VMEM((NY, 32, HD), BF),
            pltpu.VMEM((NZ, 8, HD), F32),
            pltpu.VMEM((NZ, 8, HD), F32),
            pltpu.VMEM((NG, 8, DH), F32),
            pltpu.VMEM((NG, 8, DH), F32),
            dma((3, NG)), dma((3, NG)), dma((3, NG)), dma((3, NG)), dma((NG,)), dma((NG,)),
            dma, dma, dma((NY,)), dma((NY,)), dma((NZ,)), dma((NZ,)), dma((NG,)), dma((NG,)),
        ],
        compiler_params=pltpu.CompilerParams(
            collective_id=0, has_side_effects=True, vmem_limit_bytes=48 * 1024 * 1024
        ),
    )(owners, slots, lengths, projected[0], out_grad[0], w_out)
    return (bo[None], pg[None], dw)


def solution(mesh):
    return jax.shard_map(
        per_device,
        mesh=mesh,
        in_specs=(
            P("col", "grp", None),
            P("col", "grp", None),
            P(),
            P("col", "grp"),
            P("col", "grp"),
            P("col", "grp"),
        ),
        out_specs=(P("col", "grp", None), P("col", "grp", None), P("grp", "col")),
        check_vma=False,
    )
```

time: 803 us -> 111 us (0.14)
  waiting for transfers between devices: 713 us -> 0 us
  Pallas kernels: 0 us -> 104 us
  starting transfers between devices: 35.8 us -> 0 us
  local copies, waits for them, and re-layouts: 21.4 us -> 6.11 us
  between operations: 15.1 us -> 0.67 us
  matrix products: 11.1 us -> 0 us
    unnamed x3 -> x0, waiting for transfers between devices: 475 us -> none
    reduce_scatter x1 -> x0, waiting for transfers between devices: 171 us -> none  [per_device(): lax.psum_scatter(transposed_product(mixed_rows, upstream), 'grp', scatter...]
    pallas_call x0 -> x1, Pallas kernels: none -> 104 us  [per_device(): pl.pallas_call(kernel, out_shape=(jax.ShapeDtypeStruct((ROWS, 512), BF),...]
    all_to_all x5 -> x0, waiting for transfers between devices: 66.5 us -> none  [the longest x1 42.2 us: per_device(): lax.all_to_all(sent, 'grp', split_axis=0, concat_axis=0, tiled=True)]
    all_to_all x5 -> x0, starting transfers between devices: 35.7 us -> none  [the longest x1 17 us: per_device(): lax.all_to_all(send_slots, 'grp', split_axis=0, concat_axis=0, tiled=True)]
    dot_general x9 -> x0, matrix products: 11.1 us -> none  [the longest x6 7.24 us: score_product(): return jnp.einsum(form, left, right, preferred_element_type=jnp.float32)]
    gather x9 -> x0, local copies, waits for them, and re-layouts: 9.6 us -> none  [the longest x1 1.68 us: per_device(): grads.reshape(count, block_rows, width)[arrived_slots]]
  transfers between devices with their start and end apart: 7 -> 0, of which waited for: 6 -> 0; matrix products, arithmetic and copies ran while one was open for 3% -> 0% of each run, Pallas kernels for 0% -> 0%
where the time goes in v1:
time: 111 us
  Pallas kernels  104 us (94%)
  local copies, waits for them, and re-layouts  6.11 us (6%)
    pallas_call x1, Pallas kernels, per_device(): pl.pallas_call(kernel, out_shape=(jax.ShapeDtypeStruct((ROWS, 512), BF),...  104 us
    unnamed x15, local copies, waits for them, and re-layouts  6.11 us

profile of v1, /device:TPU:1, one launch (start us, length us, event | category | flops | bytes accessed | tf_op | source)
XLA Modules:
  0.0 110.9 jit_solution(10544581557149923317)
XLA Ops:
  0.6 0.0 copy-start.3
  0.6 0.0 copy-start.4
  0.7 0.0 copy-start.5
  0.7 0.6 copy-done.3
  1.3 0.0 copy-done.4
  1.3 0.0 copy-done.5
  1.3 0.0 copy-start
  1.3 1.2 %copy-done = bf16[1,144,3072]{2,1,0:T(8,128)(2,1)S(1)} copy-done((bf16[1,144,3072]{2,1,0:T(8,128)(2,1)S(1)}, bf16[1,144,3072]{2,1,0:T(8,128)(2,1)}, u32[]{:S(2)}) %copy-start) | copy-done | bytes 884760
  2.5 0.0 copy-start.1
  2.5 1.1 %copy-done.1 = bf16[768,512]{1,0:T(8,128)(2,1)S(1)} copy-done((bf16[768,512]{1,0:T(8,128)(2,1)S(1)}, bf16[768,512]{1,0:T(8,128)(2,1)}, u32[]{:S(2)}) %copy-start.1) | copy-done | bytes 786456
  3.6 0.0 copy-start.2
  3.6 0.9 copy-done.2
  4.5 104.2 %shard_map.85 = (bf16[144,512]{1,0:T(8,128)(2,1)S(1)}, bf16[144,3072]{1,0:T(8,128)(2,1)S(1)}, f32[64,8]{1,0:T(8,128)S(1)}) custom-call(s32[1,12]{1,0:T(1,128)S(1)} %copy-done.3, s32[1,12]{1,0:T(1,128)S(1)} %copy-done.4, s32[1,12]{1,0:T(1,128)S(1)} %copy-done.5, bf16[144,3072]{1,0:T(8,128)(2,1)S(1)} %bitcast.5, bf16[144,512]{1,0:T(8,128)(2,1)S(1)} %bitcast.7, ...), custom_call_target="tpu_custom_call" | custom-call | tf_op jit(solution)/shard_map/pallas_call | solution.py:411
  108.7 0.7 copy.9
  109.4 0.7 copy.12
  110.0 0.9 copy.13
Async XLA Ops:
  0.6 0.7 copy-start.3
  0.6 0.7 copy-start.4
  0.7 0.7 copy-start.5
  1.3 1.2 %copy-start = (bf16[1,144,3072]{2,1,0:T(8,128)(2,1)S(1)}, bf16[1,144,3072]{2,1,0:T(8,128)(2,1)}, u32[]{:S(2)}) copy-start(bf16[1,144,3072]{2,1,0:T(8,128)(2,1)} %param.6) | copy-start | bytes 2654212
  2.5 1.1 %copy-start.1 = (bf16[768,512]{1,0:T(8,128)(2,1)S(1)}, bf16[768,512]{1,0:T(8,128)(2,1)}, u32[]{:S(2)}) copy-start(bf16[768,512]{1,0:T(8,128)(2,1)} %w_ref.1) | copy-start | bytes 2359300
  3.6 0.9 copy-start.2

commit v2 on v1

v2 whole, which is shorter than its diff:
```python
import functools
import math

import jax
import jax.numpy as jnp
from jax import lax
from jax.experimental import pallas as pl
from jax.experimental.pallas import tpu as pltpu
from jax.sharding import PartitionSpec as P

DH = 128
HEADS = 6
HD = 768
BR = 12
PR = 16
NG = 12
NX, NH = 4, 3
NZ, NY, NC = 4, 8, 2
ROWS = BR * NG
PROWS = PR * NG
MESH = pl.DeviceIdType.MESH
BF = jnp.bfloat16
F32 = jnp.float32


def mm(a, b):
    return lax.dot_general(a, b, (((1,), (0,)), ((), ())), preferred_element_type=F32)


def mm_nt(a, b):
    return lax.dot_general(a, b, (((1,), (1,)), ((), ())), preferred_element_type=F32)


def mm_tn(a, b):
    return lax.dot_general(a, b, (((0,), (0,)), ((), ())), preferred_element_type=F32)


def onehot(cond):
    return jnp.where(cond, 1.0, 0.0).astype(BF)


def iota(shape, dim):
    return lax.broadcasted_iota(jnp.int32, shape, dim)


def fold_in(mats, natural, folded):
    parts = [mm(mats[b], folded) for b in range(3)]
    count = folded.shape[1] // DH
    extra = [parts[b][:, head(m)] for m in range(count) for b in range(3)]
    wide = 3 * DH * count
    done = natural[:, :wide] + jnp.concatenate(extra, axis=1)
    if natural.shape[1] > wide:
        done = jnp.concatenate([done, natural[:, wide:]], axis=1)
    return done.astype(BF)


def fold_out(mats, chunk, count):
    total = None
    for b in range(3):
        lanes = [chunk[:, head(3 * m + b)] for m in range(count)]
        term = mm(mats[b], lanes[0] if count == 1 else jnp.concatenate(lanes, axis=1))
        total = term if total is None else total + term
    return total


def head(h):
    return slice(h * DH, (h + 1) * DH)


def kernel(
    own_s, slot_s, len_s, x_hbm, og_hbm, w_hbm,
    bo_ref, pg_ref, dw_ref, x_ref, og_ref, w_ref, in_sem,
    c0s, c1s, c2s, c3s, c0r, c1r, c2r, c3r, r0s, r1s, r2s, r0r, r1r, r2r,
    ts, tr, p_scr, f_scr, ogt_ref, d1s, d1r, d2s, d2r, d3s, d3r, d4s, d4r,
    c_ssem, c_rsem, r_ssem, r_rsem, t_ssem, t_rsem,
    d1_ssem, d1_rsem, d2_ssem, d2_rsem, d3_ssem, d3_rsem, d4_ssem, d4_rsem,
):
    g = lax.axis_index("grp")
    col = lax.axis_index("col")
    gx, gz = g // NH, lax.rem(g, NH)
    cs, cr = (c0s, c1s, c2s, c3s), (c0r, c1r, c2r, c3r)
    rs, rr = (r0s, r1s, r2s), (r0r, r1r, r2r)
    core = lax.rem(col, NC)
    y = lax.rem(col // NC, NY)
    zl = col // (NC * NY)

    def col_of(z_, y_, c_):
        return (z_ * NY + y_) * NC + c_

    other = col_of(zl, y, 1 - core)

    half = 2 * HD
    loads = [
        pltpu.make_async_copy(x_hbm.at[:, half:], x_ref.at[:, half:], in_sem.at[0]),
        pltpu.make_async_copy(x_hbm.at[:, :half], x_ref.at[:, :half], in_sem.at[1]),
        pltpu.make_async_copy(og_hbm, og_ref, in_sem.at[2]),
        pltpu.make_async_copy(w_hbm, w_ref, in_sem.at[3]),
    ]

    barrier = pltpu.get_barrier_semaphore()

    def greet(k, c):
        pl.semaphore_signal(
            barrier, inc=1, device_id=(lax.rem(g + k, NG), col), device_id_type=MESH
        )
        return c

    lax.fori_loop(1, NG, greet, 0)
    pl.semaphore_signal(barrier, inc=1, device_id=(g, other), device_id_type=MESH)

    def greet_y(k, c):
        pl.semaphore_signal(
            barrier, inc=1, device_id=(g, col_of(zl, lax.rem(y + k, NY), core)), device_id_type=MESH
        )
        return c

    lax.fori_loop(1, NY, greet_y, 0)

    def z_peer(k):
        place = lax.rem(zl * NH + gz + k, NG)
        return place, (gx * NH + lax.rem(place, NH), col_of(place // NH, y, core))

    def greet_z(k, c):
        pl.semaphore_signal(barrier, inc=1, device_id=z_peer(k)[1], device_id_type=MESH)
        return c

    lax.fori_loop(1, NG, greet_z, 0)
    for load in loads:
        load.start()

    def grp_copy(src, dst, ssem, rsem, k):
        peer = lax.rem(g + k, NG)
        return pltpu.make_async_remote_copy(
            src_ref=src.at[peer], dst_ref=dst.at[g], send_sem=ssem.at[peer], recv_sem=rsem.at[g],
            device_id=(peer, col), device_id_type=MESH,
        )

    def grp_start(src, dst, ssem, rsem):
        def body(k, c):
            grp_copy(src, dst, ssem, rsem, k).start()
            return c

        lax.fori_loop(1, NG, body, 0)

    def grp_wait_recv(src, dst, ssem, rsem):
        def body(k, c):
            peer = lax.rem(g + k, NG)
            pltpu.make_async_remote_copy(
                src_ref=src.at[peer], dst_ref=dst.at[peer], send_sem=ssem.at[peer],
                recv_sem=rsem.at[peer], device_id=(peer, col), device_id_type=MESH,
            ).wait_recv()
            return c

        lax.fori_loop(1, NG, body, 0)

    def grp_wait_send(src, dst, ssem, rsem):
        def body(k, c):
            grp_copy(src, dst, ssem, rsem, k).wait_send()
            return c

        lax.fori_loop(1, NG, body, 0)

    lane = iota((8, ROWS), 1)
    own_c = jnp.zeros((8, ROWS), jnp.int32)
    in_c = lane
    for j in range(NG):
        own_c = jnp.where(lane >= BR * j, own_s[0, j], own_c)
        in_c = jnp.where(lane >= BR * j, lane - BR * j, in_c)
    own_c, in_c = own_c[:1], in_c[:1]
    rows = iota((PROWS, ROWS), 0)
    same = (rows >> 4) == own_c
    in_r = rows & 15
    send_nat = onehot(same & (in_r == in_c))
    send_fold = [onehot(same & (in_r - BR + 4 * b == in_c) & (in_r >= BR)) for b in range(3)]

    def put(i, chunk):
        cs[i][...] = chunk.reshape(NG, PR, chunk.shape[1])
        cr[i][g] = cs[i][g]

    def send(i):
        grp_start(cs[i], cr[i], c_ssem.at[i], c_rsem.at[i])

    loads[0].wait()
    q = x_ref[:, 2 * HD : 3 * HD]
    put(0, fold_in(send_fold, mm(send_nat, q), x_ref[:, 3 * HD : 3 * HD + 2 * DH]))
    for o in range(NG):
        tile = jnp.zeros((1, DH), jnp.int32)
        for j in range(NG):
            tile = jnp.where(jnp.full((1, DH), own_s[0, j]) == o, slot_s[0, j], tile)
        ts[o] = tile.astype(F32)
    tr[g] = ts[g]

    pl.semaphore_wait(barrier, NG - 1 + 1 + NY - 1 + NG - 1)

    grp_start(ts, tr, t_ssem, t_rsem)
    send(0)
    loads[1].wait()
    nat = jnp.concatenate([x_ref[:, 3 * HD + 2 * DH : 4 * HD], x_ref[:, HD : HD + 2 * DH]], axis=1)
    put(1, fold_in(send_fold, mm(send_nat, nat), x_ref[:, HD + 2 * DH : HD + 4 * DH]))
    send(1)
    loads[2].wait()
    loads[3].wait()
    branch = mm_nt(og_ref[...], w_ref[...]).astype(BF).astype(F32)
    gate = x_ref[:, :HD].astype(F32)
    grad = (branch * gate).astype(BF)
    put(
        2,
        fold_in(
            send_fold,
            mm(send_nat, jnp.concatenate([x_ref[:, HD + 4 * DH : half], grad[:, head(0)]], axis=1)),
            grad[:, head(1)],
        ),
    )
    send(2)
    put(3, fold_in(send_fold, mm(send_nat, grad[:, 2 * DH : 5 * DH]), grad[:, head(5)]))
    send(3)

    ogt = jnp.transpose(og_ref[...].astype(F32))
    for cc in range(NC):
        ogt_ref[cc] = jnp.concatenate(
            [
                ogt[((zz * NY + yy) * NC + cc) * 8 : ((zz * NY + yy) * NC + cc) * 8 + 8]
                for yy in range(NY)
                for zz in range(NZ)
            ],
            axis=0,
        ).astype(BF)

    rows = iota((PROWS, PROWS), 0)
    cols = iota((PROWS, PROWS), 1)
    same = (rows >> 4) == (cols >> 4)
    rr_, cc_ = rows & 15, cols & 15
    unfold = [onehot(same & (cc_ >= BR) & (rr_ == cc_ - BR + 4 * b)) for b in range(3)]
    infold = [onehot(same & (rr_ >= BR) & (cc_ == rr_ - BR + 4 * b)) for b in range(3)]

    rows = iota((ROWS, PROWS), 0)
    cols = iota((ROWS, PROWS), 1)
    own_r = jnp.zeros((ROWS, PROWS), jnp.int32)
    in_b = rows
    for j in range(NG):
        own_r = jnp.where(rows >= BR * j, own_s[0, j], own_r)
        in_b = jnp.where(rows >= BR * j, rows - BR * j, in_b)
    same = own_r == (cols >> 4)
    cc_ = cols & 15
    home_nat = onehot(same & (cc_ == in_b))
    home_fold = [onehot(same & (cc_ >= BR) & (cc_ - BR + 4 * b == in_b)) for b in range(3)]

    grp_wait_recv(ts, tr, t_ssem, t_rsem)
    slot_r = jnp.concatenate([jnp.broadcast_to(tr[d], (PR, DH)) for d in range(NG)], axis=0)
    lane = iota((8, PROWS), 1)
    slot_c = jnp.zeros((8, PROWS), F32)
    for d in range(NG):
        slot_c = jnp.where((lane >> 4) == d, jnp.broadcast_to(tr[d][:, :1], (8, PROWS)), slot_c)
    first = jnp.int32(0)
    length = jnp.int32(1)
    first_r, len_r = jnp.zeros((PROWS, DH), F32), jnp.ones((PROWS, DH), F32)
    first_c = jnp.zeros((8, PROWS), F32)
    for s in range(NG):
        start = len_s[0, s]
        opened = start > 0
        first = jnp.where(opened, s, first)
        length = jnp.where(opened, start, length)
        first_f, length_f = first.astype(F32), length.astype(F32)
        first_r = jnp.where(slot_r == float(s), first_f, first_r)
        len_r = jnp.where(slot_r == float(s), length_f, len_r)
        first_c = jnp.where(slot_c == float(s), first_f, first_c)
    sub = iota((PROWS, DH), 0) & 15
    pos_r = (slot_r - first_r) * BR + sub.astype(F32)
    valid_r = (pos_r < len_r) & (sub < BR)
    pos_c = (slot_c - first_c) * BR + (lane & 15).astype(F32)
    pos_c = jnp.where((lane & 15) < BR, pos_c, 1e9)
    inv_r = jnp.where(valid_r, 1.0 / len_r, 0.0)
    valid = jnp.where(valid_r, 1.0, 0.0)[:, :1]
    weight = jnp.where(
        (first_r[:, :1] == first_c[:1]) & (pos_c[:1] <= pos_r[:, :1]), inv_r[:, :1], 0.0
    )

    scale = 1.0 / math.sqrt(DH)

    def chunk_in(i):
        grp_wait_recv(cs[i], cr[i], c_ssem.at[i], c_rsem.at[i])
        return cr[i][...].reshape(PROWS, cr[i].shape[2])

    c0 = chunk_in(0)
    k01 = fold_out(unfold, c0, 2).astype(BF)
    qs = [c0[:, head(h)] for h in range(HEADS)]

    def scores(h, kh):
        s = mm_nt(qs[h], kh) * scale
        sig = jax.nn.sigmoid(s)
        p_scr[h] = (s * sig * weight).astype(BF)
        f_scr[h] = sig * (1.0 + s * (1.0 - sig)) * weight

    scores(0, k01[:, :DH])
    scores(1, k01[:, DH:])
    c1 = chunk_in(1)
    ks = [k01[:, :DH], k01[:, DH:]] + [c1[:, head(h)] for h in range(4)]
    for h in range(2, HEADS):
        scores(h, ks[h])
    v23 = fold_out(unfold, c1, 2).astype(BF)
    vs = [c1[:, head(4)], c1[:, head(5)], v23[:, :DH], v23[:, DH:]]
    attended = [mm(p_scr[h], vs[h]) for h in range(4)]
    c2 = chunk_in(2)
    grad1 = fold_out(unfold, c2, 1)
    vs += [c2[:, head(0)], c2[:, head(1)]]
    attended += [mm(p_scr[h], vs[h]) for h in range(4, HEADS)]
    att = jnp.concatenate(attended, axis=1)
    centre = jnp.mean(att, axis=1, keepdims=True)
    att = att - centre
    rstd = lax.rsqrt(jnp.mean(att * att, axis=1, keepdims=True) + 1e-05)
    normed = att * rstd

    def back(i, natural, folded):
        rs[i][...] = fold_in(infold, natural, folded.astype(BF)).reshape(NG, PR, natural.shape[1])
        rr[i][g] = rs[i][g]

    def back_start(i):
        grp_start(rs[i], rr[i], r_ssem.at[i], r_rsem.at[i])

    def back_chain(i):
        def body(k, c):
            grp_copy(rs[i - 1], rr[i - 1], r_ssem.at[i - 1], r_rsem.at[i - 1], k).wait_send()
            grp_copy(rs[i], rr[i], r_ssem.at[i], r_rsem.at[i], k).start()
            return c

        lax.fori_loop(1, NG, body, 0)

    def back_sent(i):
        grp_wait_send(rs[i], rr[i], r_ssem.at[i], r_rsem.at[i])

    back(0, jnp.concatenate([normed[:, : 3 * DH], normed[:, 4 * DH :]], axis=1), normed[:, head(3)])

    back_start(0)

    c3 = chunk_in(3)
    gr = jnp.concatenate(
        [c2[:, head(2)].astype(F32), grad1, c3.astype(F32), fold_out(unfold, c3, 1)], axis=1
    )
    datt = rstd * (
        gr - jnp.mean(gr, axis=1, keepdims=True)
        - normed * jnp.mean(gr * normed, axis=1, keepdims=True)
    )
    datt = jnp.where(valid > 0.5, datt, 0.0).astype(BF)

    def dv(h):
        return mm_tn(p_scr[h], datt[:, head(h)])

    def dqk(h):
        ds = (mm_nt(datt[:, head(h)], vs[h]) * f_scr[h]).astype(BF)
        return [mm(ds, ks[h]) * scale, mm_tn(ds, qs[h]) * scale]

    for i in (1, 2):
        a = 3 * (i - 1)
        natural = dqk(a) + dqk(a + 1) + dqk(a + 2) + [dv(a)]
        back(i, jnp.concatenate(natural, axis=1), jnp.concatenate([dv(a + 1), dv(a + 2)], axis=1))
        if i == 1:
            back_chain(1)

    def chunk_home(i):
        grp_wait_recv(rs[i], rr[i], r_ssem.at[i], r_rsem.at[i])
        chunk = rr[i][...].reshape(PROWS, rr[i].shape[2])
        return mm(home_nat, chunk), chunk

    n_part, chunk = chunk_home(0)
    n_home = jnp.concatenate(
        [n_part[:, : 3 * DH], fold_out(home_fold, chunk, 1), n_part[:, 3 * DH :]], axis=1
    )
    z = (n_home * gate).astype(BF)

    zc = jnp.concatenate(
        [z[:, 192 * xx : 192 * xx + DH] for xx in range(NX)]
        + [z[:, 192 * xx + DH : 192 * xx + 192] for xx in range(NX)],
        axis=1,
    )
    d1s[...] = mm(ogt_ref[1 - core], zc).astype(BF)
    d1 = pltpu.make_async_remote_copy(
        src_ref=d1s, dst_ref=d1r, send_sem=d1_ssem, recv_sem=d1_rsem,
        device_id=(g, other), device_id_type=MESH,
    )
    d1.start()
    own = mm(ogt_ref[core], zc)
    d1.wait_recv()
    mine = (own + d1r[...].astype(F32)).astype(BF)
    for xx in range(NX):
        d2s[xx, :256] = mine[:, head(xx)]
        tail = mine[:, 512 + 64 * xx : 576 + 64 * xx]
        d2s[xx, 256:] = jnp.concatenate([tail[:128], tail[128:]], axis=1)

    def d2(k, slot):
        peer = lax.rem(gx + k, NX)
        return pltpu.make_async_remote_copy(
            src_ref=d2s.at[peer], dst_ref=d2r.at[peer if slot else gx], send_sem=d2_ssem.at[peer],
            recv_sem=d2_rsem.at[peer if slot else gx],
            device_id=(peer * NH + gz, col), device_id_type=MESH,
        )

    def d2_start(k, c):
        d2(k, False).start()
        return c

    lax.fori_loop(1, NX, d2_start, 0)
    back_chain(2)
    d2r[gx] = d2s[gx]
    branch = mm_nt(og_ref[...], w_ref[...]).astype(BF).astype(F32)
    pg_ref[:, :HD] = (branch * n_home).astype(BF)
    bo_ref[...] = mm(z, w_ref[...]).astype(BF)

    def d2_wait(k, c):
        d2(k, True).wait_recv()
        return c

    lax.fori_loop(1, NX, d2_wait, 0)
    total = d2r[0].astype(F32)
    for xx in range(1, NX):
        total = total + d2r[xx].astype(F32)
    for yy in range(NY):
        d3s[yy, :32] = total[32 * yy : 32 * yy + 32].astype(BF)
        row, lane0 = 256 + 32 * (yy % 4), 64 * (yy // 4)
        tail = total[row : row + 32, lane0 : lane0 + 64]
        d3s[yy, 32:] = jnp.concatenate([tail[:16], tail[16:]], axis=1).astype(BF)

    def d3(k, slot):
        peer = lax.rem(y + k, NY)
        return pltpu.make_async_remote_copy(
            src_ref=d3s.at[peer], dst_ref=d3r.at[peer if slot else y], send_sem=d3_ssem.at[peer],
            recv_sem=d3_rsem.at[peer if slot else y],
            device_id=(g, col_of(zl, peer, core)), device_id_type=MESH,
        )

    def d3_start(k, c):
        d3(k, False).start()
        return c

    lax.fori_loop(1, NY, d3_start, 0)
    d3r[y] = d3s[y]

    def d3_wait(k, c):
        d3(k, True).wait_recv()
        return c

    lax.fori_loop(1, NY, d3_wait, 0)
    total = d3r[0].astype(F32)
    for yy in range(1, NY):
        total = total + d3r[yy].astype(F32)
    for zz in range(NZ):
        for hh in range(NH):
            row, lane0 = (8 * zz, 64 * hh) if hh < 2 else (32 + 8 * (zz % 2), 64 * (zz // 2))
            d4s[zz * NH + hh, :, :64] = total[row : row + 8, lane0 : lane0 + 64]
            d4s[zz * NH + hh, :, 64:] = jnp.zeros((8, 64), F32)
    place = zl * NH + gz

    def d4(k, slot):
        peer, device = z_peer(k)
        return pltpu.make_async_remote_copy(
            src_ref=d4s.at[peer], dst_ref=d4r.at[peer if slot else place], send_sem=d4_ssem.at[peer],
            recv_sem=d4_rsem.at[peer if slot else place], device_id=device, device_id_type=MESH,
        )

    def d4_start(k, c):
        d4(k, False).start()
        return c

    lax.fori_loop(1, NG, d4_start, 0)
    d4r[place] = d4s[place]

    for i in (1, 2):
        a = 3 * (i - 1)
        part, chunk = chunk_home(i)
        part = part.astype(BF)
        for h in range(3):
            lo = 2 * HD + (a + h) * DH
            pg_ref[:, lo : lo + DH] = part[:, head(2 * h)]
            pg_ref[:, lo + HD : lo + HD + DH] = part[:, head(2 * h + 1)]
        lo = HD + a * DH
        pg_ref[:, lo : lo + DH] = part[:, head(6)]
        pg_ref[:, lo + DH : lo + 3 * DH] = fold_out(home_fold, chunk, 2).astype(BF)

    def d4_wait(k, c):
        d4(k, True).wait_recv()
        return c

    lax.fori_loop(1, NG, d4_wait, 0)
    total = d4r[0]
    for o in range(1, NG):
        total = total + d4r[o]
    dw_ref[...] = total[:, :64]

    grp_wait_send(ts, tr, t_ssem, t_rsem)
    for i in range(4):
        grp_wait_send(cs[i], cr[i], c_ssem.at[i], c_rsem.at[i])
    back_sent(2)
    d1.wait_send()

    def d2_sent(k, c):
        d2(k, False).wait_send()
        return c

    lax.fori_loop(1, NX, d2_sent, 0)

    def d3_sent(k, c):
        d3(k, False).wait_send()
        return c

    lax.fori_loop(1, NY, d3_sent, 0)

    def d4_sent(k, c):
        d4(k, False).wait_send()
        return c

    lax.fori_loop(1, NG, d4_sent, 0)


def per_device(projected, out_grad, w_out, owners, slots, lengths):
    dma = pltpu.SemaphoreType.DMA
    vmem = pl.BlockSpec(memory_space=pltpu.VMEM)
    hbm = pl.BlockSpec(memory_space=pltpu.HBM)
    smem = pl.BlockSpec(memory_space=pltpu.SMEM)
    bo, pg, dw = pl.pallas_call(
        kernel,
        out_shape=(
            jax.ShapeDtypeStruct((ROWS, 512), BF),
            jax.ShapeDtypeStruct((ROWS, 4 * HD), BF),
            jax.ShapeDtypeStruct((8, 64), F32),
        ),
        in_specs=[smem, smem, smem, hbm, hbm, hbm],
        out_specs=(vmem, vmem, vmem),
        scratch_shapes=[
            pltpu.VMEM((ROWS, 4 * HD), BF),
            pltpu.VMEM((ROWS, 512), BF),
            pltpu.VMEM((HD, 512), BF),
            dma((4,)),
            *[pltpu.VMEM((NG, PR, w), BF) for w in (768, 768, 384, 384) * 2 + (640, 896, 896) * 2],
            pltpu.VMEM((NG, 1, DH), F32),
            pltpu.VMEM((NG, 1, DH), F32),
            pltpu.VMEM((HEADS, PROWS, PROWS), BF),
            pltpu.VMEM((HEADS, PROWS, PROWS), F32),
            pltpu.VMEM((NC, 256, ROWS), BF),
            pltpu.VMEM((256, HD), BF),
            pltpu.VMEM((256, HD), BF),
            pltpu.VMEM((NX, 384, DH), BF),
            pltpu.VMEM((NX, 384, DH), BF),
            pltpu.VMEM((NY, 48, DH), BF),
            pltpu.VMEM((NY, 48, DH), BF),
            pltpu.VMEM((NG, 8, DH), F32),
            pltpu.VMEM((NG, 8, DH), F32),
            dma((4, NG)), dma((4, NG)), dma((3, NG)), dma((3, NG)), dma((NG,)), dma((NG,)),
            dma, dma, dma((NX,)), dma((NX,)), dma((NY,)), dma((NY,)), dma((NG,)), dma((NG,)),
        ],
        compiler_params=pltpu.CompilerParams(
            collective_id=0, has_side_effects=True, vmem_limit_bytes=63 * 1024 * 1024
        ),
    )(owners, slots, lengths, projected[0], out_grad[0], w_out)
    return (bo[None], pg[None], dw.T)


def solution(mesh):
    return jax.shard_map(
        per_device,
        mesh=mesh,
        in_specs=(
            P("col", "grp", None),
            P("col", "grp", None),
            P(),
            P("col", "grp"),
            P("col", "grp"),
            P("col", "grp"),
        ),
        out_specs=(P("col", "grp", None), P("col", "grp", None), P("grp", "col")),
        check_vma=False,
    )
```

time: 111 us -> 97.9 us (0.88)
  Pallas kernels: 104 us -> 92.7 us
  local copies, waits for them, and re-layouts: 6.11 us -> 4.31 us
    pallas_call x1, Pallas kernels: 104 us -> 92.7 us  [per_device(): pl.pallas_call(kernel, out_shape=(jax.ShapeDtypeStruct((ROWS, 512), BF),...]
    unnamed x15 -> x5, local copies, waits for them, and re-layouts: 6.11 us -> 4.31 us
where the time goes in v2:
time: 97.9 us; the launch traced here: 97.7 us
  Pallas kernels  92.7 us (95%)
  local copies, waits for them, and re-layouts  4.31 us (4%)
    pallas_call x1, Pallas kernels, per_device(): pl.pallas_call(kernel, out_shape=(jax.ShapeDtypeStruct((ROWS, 512), BF),...  92.7 us
    unnamed x5, local copies, waits for them, and re-layouts  4.31 us

profile of v2, /device:TPU:1, one launch (start us, length us, event | category | flops | bytes accessed | tf_op | source)
XLA Modules:
  0.0 97.7 jit_solution(451044779047204049)
XLA Ops:
  0.6 92.7 %shard_map.85 = (bf16[144,512]{1,0:T(8,128)(2,1)}, bf16[144,3072]{1,0:T(8,128)(2,1)}, f32[8,64]{1,0:T(8,128)}) custom-call(s32[1,12]{1,0:T(1,128)} %own_s.1, s32[1,12]{1,0:T(1,128)} %slot_s.1, s32[1,12]{1,0:T(1,128)} %len_s.1, bf16[144,3072]{1,0:T(8,128)(2,1)} %bitcast.6, bf16[144,512]{1,0:T(8,128)(2,1)} %bitcast.8, bf16[768,512]{1,0:T(8,128)(2,1)} %w_hbm.1), custom_call_target="tpu_custom_call" | custom-call | tf_op jit(solution)/shard_map/pallas_call | solution.py:518
  93.4 1.6 %copy.12 = bf16[1,144,512]{2,1,0:T(8,128)(2,1)} copy(bf16[1,144,512]{2,1,0:T(8,128)(2,1)} %bitcast.7) | data formatting | bytes 294912
  94.9 0.0 copy-start
  94.9 2.1 %copy.13 = bf16[1,144,3072]{2,1,0:T(8,128)(2,1)} copy(bf16[1,144,3072]{2,1,0:T(8,128)(2,1)} %bitcast.5) | data formatting | bytes 1769472
  97.1 0.0 copy-done
  97.1 0.6 copy.14
Async XLA Ops:
  94.9 2.1 %copy-start = (f32[8,64]{1,0:T(8,128)S(1)}, f32[8,64]{1,0:T(8,128)}, u32[]{:S(2)}) copy-start(f32[8,64]{1,0:T(8,128)} %get-tuple-element.8) | copy-start | bytes 6148

commit v3 on v2

--- a/solution.py
+++ b/solution.py
@@ -198,33 +198,16 @@
     nat = jnp.concatenate([x_ref[:, 3 * HD + 2 * DH : 4 * HD], x_ref[:, HD : HD + 2 * DH]], axis=1)
     put(1, fold_in(send_fold, mm(send_nat, nat), x_ref[:, HD + 2 * DH : HD + 4 * DH]))
     send(1)
+    nat = jnp.concatenate([x_ref[:, HD + 4 * DH : half], x_ref[:, :DH]], axis=1)
+    put(2, fold_in(send_fold, mm(send_nat, nat), x_ref[:, DH : 2 * DH]))
+    send(2)
     loads[2].wait()
+    nat = jnp.concatenate([x_ref[:, 2 * DH : HD], og_ref[:, : 2 * DH]], axis=1)
+    put(3, fold_in(send_fold, mm(send_nat, nat), og_ref[:, 2 * DH :]))
+    send(3)
     loads[3].wait()
     branch = mm_nt(og_ref[...], w_ref[...]).astype(BF).astype(F32)
     gate = x_ref[:, :HD].astype(F32)
-    grad = (branch * gate).astype(BF)
-    put(
-        2,
-        fold_in(
-            send_fold,
-            mm(send_nat, jnp.concatenate([x_ref[:, HD + 4 * DH : half], grad[:, head(0)]], axis=1)),
-            grad[:, head(1)],
-        ),
-    )
-    send(2)
-    put(3, fold_in(send_fold, mm(send_nat, grad[:, 2 * DH : 5 * DH]), grad[:, head(5)]))
-    send(3)
-
-    ogt = jnp.transpose(og_ref[...].astype(F32))
-    for cc in range(NC):
-        ogt_ref[cc] = jnp.concatenate(
-            [
-                ogt[((zz * NY + yy) * NC + cc) * 8 : ((zz * NY + yy) * NC + cc) * 8 + 8]
-                for yy in range(NY)
-                for zz in range(NZ)
-            ],
-            axis=0,
-        ).astype(BF)
 
     rows = iota((PROWS, PROWS), 0)
     cols = iota((PROWS, PROWS), 1)
@@ -301,7 +284,7 @@
     vs = [c1[:, head(4)], c1[:, head(5)], v23[:, :DH], v23[:, DH:]]
     attended = [mm(p_scr[h], vs[h]) for h in range(4)]
     c2 = chunk_in(2)
-    grad1 = fold_out(unfold, c2, 1)
+    gate1 = fold_out(unfold, c2, 1)
     vs += [c2[:, head(0)], c2[:, head(1)]]
     attended += [mm(p_scr[h], vs[h]) for h in range(4, HEADS)]
     att = jnp.concatenate(attended, axis=1)
@@ -317,25 +300,36 @@
     def back_start(i):
         grp_start(rs[i], rr[i], r_ssem.at[i], r_rsem.at[i])
 
-    def back_chain(i):
-        def body(k, c):
-            grp_copy(rs[i - 1], rr[i - 1], r_ssem.at[i - 1], r_rsem.at[i - 1], k).wait_send()
-            grp_copy(rs[i], rr[i], r_ssem.at[i], r_rsem.at[i], k).start()
-            return c
-
-        lax.fori_loop(1, NG, body, 0)
-
-    def back_sent(i):
-        grp_wait_send(rs[i], rr[i], r_ssem.at[i], r_rsem.at[i])
-
     back(0, jnp.concatenate([normed[:, : 3 * DH], normed[:, 4 * DH :]], axis=1), normed[:, head(3)])
 
     back_start(0)
 
     c3 = chunk_in(3)
-    gr = jnp.concatenate(
-        [c2[:, head(2)].astype(F32), grad1, c3.astype(F32), fold_out(unfold, c3, 1)], axis=1
+    gate_o = jnp.concatenate(
+        [c2[:, head(2)].astype(F32), gate1, c3[:, : 4 * DH].astype(F32)], axis=1
     )
+    og_o = jnp.concatenate([c3[:, 4 * DH :], fold_out(unfold, c3, 2).astype(BF)], axis=1)
+
+    ogt = jnp.transpose(og_o.astype(F32))
+    for cc in range(NC):
+        ogt_ref[cc] = jnp.concatenate(
+            [
+                ogt[((zz * NY + yy) * NC + cc) * 8 : ((zz * NY + yy) * NC + cc) * 8 + 8]
+                for yy in range(NY)
+                for zz in range(NZ)
+            ],
+            axis=0,
+        ).astype(BF)
+
+    zo = (normed * gate_o).astype(BF)
+    d1s[...] = mm(ogt_ref[1 - core], zo).astype(BF)
+    d1 = pltpu.make_async_remote_copy(
+        src_ref=d1s, dst_ref=d1r, send_sem=d1_ssem, recv_sem=d1_rsem,
+        device_id=(g, other), device_id_type=MESH,
+    )
+    d1.start()
+
+    gr = mm_nt(og_o, w_ref[...]).astype(BF).astype(F32) * gate_o
     datt = rstd * (
         gr - jnp.mean(gr, axis=1, keepdims=True)
         - normed * jnp.mean(gr * normed, axis=1, keepdims=True)
@@ -349,103 +343,76 @@
         ds = (mm_nt(datt[:, head(h)], vs[h]) * f_scr[h]).astype(BF)
         return [mm(ds, ks[h]) * scale, mm_tn(ds, qs[h]) * scale]
 
-    for i in (1, 2):
+    def back_heads(i):
         a = 3 * (i - 1)
         natural = dqk(a) + dqk(a + 1) + dqk(a + 2) + [dv(a)]
         back(i, jnp.concatenate(natural, axis=1), jnp.concatenate([dv(a + 1), dv(a + 2)], axis=1))
-        if i == 1:
-            back_chain(1)
+        back_start(i)
+
+    back_heads(1)
+    own = mm(ogt_ref[core], zo)
+    d1.wait_recv()
+    d2s[...] = (own + d1r[...].astype(F32)).astype(BF).reshape(NY, 32, HD)
+
+    def d2(k, slot):
+        peer = lax.rem(y + k, NY)
+        return pltpu.make_async_remote_copy(
+            src_ref=d2s.at[peer], dst_ref=d2r.at[peer if slot else y], send_sem=d2_ssem.at[peer],
+            recv_sem=d2_rsem.at[peer if slot else y],
+            device_id=(g, col_of(zl, peer, core)), device_id_type=MESH,
+        )
+
+    def d2_start(k, c):
+        d2(k, False).start()
+        return c
+
+    lax.fori_loop(1, NY, d2_start, 0)
+    d2r[y] = d2s[y]
+    back_heads(2)
 
     def chunk_home(i):
         grp_wait_recv(rs[i], rr[i], r_ssem.at[i], r_rsem.at[i])
         chunk = rr[i][...].reshape(PROWS, rr[i].shape[2])
         return mm(home_nat, chunk), chunk
 
-    n_part, chunk = chunk_home(0)
-    n_home = jnp.concatenate(
-        [n_part[:, : 3 * DH], fold_out(home_fold, chunk, 1), n_part[:, 3 * DH :]], axis=1
-    )
-    z = (n_home * gate).astype(BF)
-
-    zc = jnp.concatenate(
-        [z[:, 192 * xx : 192 * xx + DH] for xx in range(NX)]
-        + [z[:, 192 * xx + DH : 192 * xx + 192] for xx in range(NX)],
-        axis=1,
-    )
-    d1s[...] = mm(ogt_ref[1 - core], zc).astype(BF)
-    d1 = pltpu.make_async_remote_copy(
-        src_ref=d1s, dst_ref=d1r, send_sem=d1_ssem, recv_sem=d1_rsem,
-        device_id=(g, other), device_id_type=MESH,
-    )
-    d1.start()
-    own = mm(ogt_ref[core], zc)
-    d1.wait_recv()
-    mine = (own + d1r[...].astype(F32)).astype(BF)
+    def d2_wait(k, c):
+        d2(k, True).wait_recv()
+        return c
+
+    lax.fori_loop(1, NY, d2_wait, 0)
+    total = d2r[0].astype(F32)
+    for yy in range(1, NY):
+        total = total + d2r[yy].astype(F32)
     for xx in range(NX):
-        d2s[xx, :256] = mine[:, head(xx)]
-        tail = mine[:, 512 + 64 * xx : 576 + 64 * xx]
-        d2s[xx, 256:] = jnp.concatenate([tail[:128], tail[128:]], axis=1)
-
-    def d2(k, slot):
+        part = total[:, 192 * xx : 192 * xx + 192].astype(BF)
+        d3s[xx] = jnp.concatenate([part, part[:, :64]], axis=1)
+
+    def d3(k, slot):
         peer = lax.rem(gx + k, NX)
         return pltpu.make_async_remote_copy(
-            src_ref=d2s.at[peer], dst_ref=d2r.at[peer if slot else gx], send_sem=d2_ssem.at[peer],
-            recv_sem=d2_rsem.at[peer if slot else gx],
+            src_ref=d3s.at[peer], dst_ref=d3r.at[peer if slot else gx], send_sem=d3_ssem.at[peer],
+            recv_sem=d3_rsem.at[peer if slot else gx],
             device_id=(peer * NH + gz, col), device_id_type=MESH,
         )
 
-    def d2_start(k, c):
-        d2(k, False).start()
-        return c
-
-    lax.fori_loop(1, NX, d2_start, 0)
-    back_chain(2)
-    d2r[gx] = d2s[gx]
-    branch = mm_nt(og_ref[...], w_ref[...]).astype(BF).astype(F32)
-    pg_ref[:, :HD] = (branch * n_home).astype(BF)
-    bo_ref[...] = mm(z, w_ref[...]).astype(BF)
-
-    def d2_wait(k, c):
-        d2(k, True).wait_recv()
-        return c
-
-    lax.fori_loop(1, NX, d2_wait, 0)
-    total = d2r[0].astype(F32)
-    for xx in range(1, NX):
-        total = total + d2r[xx].astype(F32)
-    for yy in range(NY):
-        d3s[yy, :32] = total[32 * yy : 32 * yy + 32].astype(BF)
-        row, lane0 = 256 + 32 * (yy % 4), 64 * (yy // 4)
-        tail = total[row : row + 32, lane0 : lane0 + 64]
-        d3s[yy, 32:] = jnp.concatenate([tail[:16], tail[16:]], axis=1).astype(BF)
-
-    def d3(k, slot):
-        peer = lax.rem(y + k, NY)
-        return pltpu.make_async_remote_copy(
-            src_ref=d3s.at[peer], dst_ref=d3r.at[peer if slot else y], send_sem=d3_ssem.at[peer],
-            recv_sem=d3_rsem.at[peer if slot else y],
-            device_id=(g, col_of(zl, peer, core)), device_id_type=MESH,
-        )
-
     def d3_start(k, c):
         d3(k, False).start()
         return c
 
-    lax.fori_loop(1, NY, d3_start, 0)
-    d3r[y] = d3s[y]
+    lax.fori_loop(1, NX, d3_start, 0)
+    d3r[gx] = d3s[gx]
 
     def d3_wait(k, c):
         d3(k, True).wait_recv()
         return c
 
-    lax.fori_loop(1, NY, d3_wait, 0)
+    lax.fori_loop(1, NX, d3_wait, 0)
     total = d3r[0].astype(F32)
-    for yy in range(1, NY):
-        total = total + d3r[yy].astype(F32)
+    for xx in range(1, NX):
+        total = total + d3r[xx].astype(F32)
     for zz in range(NZ):
         for hh in range(NH):
-            row, lane0 = (8 * zz, 64 * hh) if hh < 2 else (32 + 8 * (zz % 2), 64 * (zz // 2))
-            d4s[zz * NH + hh, :, :64] = total[row : row + 8, lane0 : lane0 + 64]
+            d4s[zz * NH + hh, :, :64] = total[8 * zz : 8 * zz + 8, 64 * hh : 64 * hh + 64]
             d4s[zz * NH + hh, :, 64:] = jnp.zeros((8, 64), F32)
     place = zl * NH + gz
 
@@ -462,6 +429,14 @@
 
     lax.fori_loop(1, NG, d4_start, 0)
     d4r[place] = d4s[place]
+
+    n_part, chunk = chunk_home(0)
+    n_home = jnp.concatenate(
+        [n_part[:, : 3 * DH], fold_out(home_fold, chunk, 1), n_part[:, 3 * DH :]], axis=1
+    )
+    z = (n_home * gate).astype(BF)
+    pg_ref[:, :HD] = (branch * n_home).astype(BF)
+    bo_ref[...] = mm(z, w_ref[...]).astype(BF)
 
     for i in (1, 2):
         a = 3 * (i - 1)
@@ -488,20 +463,21 @@
     grp_wait_send(ts, tr, t_ssem, t_rsem)
     for i in range(4):
         grp_wait_send(cs[i], cr[i], c_ssem.at[i], c_rsem.at[i])
-    back_sent(2)
+    for i in range(3):
+        grp_wait_send(rs[i], rr[i], r_ssem.at[i], r_rsem.at[i])
     d1.wait_send()
 
     def d2_sent(k, c):
         d2(k, False).wait_send()
         return c
 
-    lax.fori_loop(1, NX, d2_sent, 0)
+    lax.fori_loop(1, NY, d2_sent, 0)
 
     def d3_sent(k, c):
         d3(k, False).wait_send()
         return c
 
-    lax.fori_loop(1, NY, d3_sent, 0)
+    lax.fori_loop(1, NX, d3_sent, 0)
 
     def d4_sent(k, c):
         d4(k, False).wait_send()
@@ -529,22 +505,22 @@
             pltpu.VMEM((ROWS, 512), BF),
             pltpu.VMEM((HD, 512), BF),
             dma((4,)),
-            *[pltpu.VMEM((NG, PR, w), BF) for w in (768, 768, 384, 384) * 2 + (640, 896, 896) * 2],
+            *[pltpu.VMEM((NG, PR, w), BF) for w in (768, 768, 384, 768) * 2 + (640, 896, 896) * 2],
             pltpu.VMEM((NG, 1, DH), F32),
             pltpu.VMEM((NG, 1, DH), F32),
             pltpu.VMEM((HEADS, PROWS, PROWS), BF),
             pltpu.VMEM((HEADS, PROWS, PROWS), F32),
-            pltpu.VMEM((NC, 256, ROWS), BF),
+            pltpu.VMEM((NC, 256, PROWS), BF),
             pltpu.VMEM((256, HD), BF),
             pltpu.VMEM((256, HD), BF),
-            pltpu.VMEM((NX, 384, DH), BF),
-            pltpu.VMEM((NX, 384, DH), BF),
-            pltpu.VMEM((NY, 48, DH), BF),
-            pltpu.VMEM((NY, 48, DH), BF),
+            pltpu.VMEM((NY, 32, HD), BF),
+            pltpu.VMEM((NY, 32, HD), BF),
+            pltpu.VMEM((NX, 32, 256), BF),
+            pltpu.VMEM((NX, 32, 256), BF),
             pltpu.VMEM((NG, 8, DH), F32),
             pltpu.VMEM((NG, 8, DH), F32),
             dma((4, NG)), dma((4, NG)), dma((3, NG)), dma((3, NG)), dma((NG,)), dma((NG,)),
-            dma, dma, dma((NX,)), dma((NX,)), dma((NY,)), dma((NY,)), dma((NG,)), dma((NG,)),
+            dma, dma, dma((NY,)), dma((NY,)), dma((NX,)), dma((NX,)), dma((NG,)), dma((NG,)),
         ],
         compiler_params=pltpu.CompilerParams(
             collective_id=0, has_side_effects=True, vmem_limit_bytes=63 * 1024 * 1024

time: 97.9 us -> 95.4 us (0.974)
  the two profiles are of different devices: /device:TPU:1 before, /device:TPU:32 now
where the time goes in v3:
time: 95.4 us; the launch traced here: 95.2 us
  Pallas kernels  90.2 us (95%)
  local copies, waits for them, and re-layouts  4.31 us (5%)
    pallas_call x1, Pallas kernels, per_device(): pl.pallas_call(kernel, out_shape=(jax.ShapeDtypeStruct((ROWS, 512), BF),...  90.2 us
    unnamed x5, local copies, waits for them, and re-layouts  4.31 us

profile of v3, /device:TPU:32, one launch (start us, length us, event | category | flops | bytes accessed | tf_op | source)
XLA Modules:
  0.0 95.2 jit_solution(17827980059687729988)
XLA Ops:
  0.6 90.2 %shard_map.85 = (bf16[144,512]{1,0:T(8,128)(2,1)}, bf16[144,3072]{1,0:T(8,128)(2,1)}, f32[8,64]{1,0:T(8,128)}) custom-call(s32[1,12]{1,0:T(1,128)} %own_s.1, s32[1,12]{1,0:T(1,128)} %slot_s.1, s32[1,12]{1,0:T(1,128)} %len_s.1, bf16[144,3072]{1,0:T(8,128)(2,1)} %bitcast.6, bf16[144,512]{1,0:T(8,128)(2,1)} %bitcast.8, bf16[768,512]{1,0:T(8,128)(2,1)} %w_hbm.1), custom_call_target="tpu_custom_call" | custom-call | tf_op jit(solution)/shard_map/pallas_call | solution.py:494
  90.8 1.6 %copy.12 = bf16[1,144,512]{2,1,0:T(8,128)(2,1)} copy(bf16[1,144,512]{2,1,0:T(8,128)(2,1)} %bitcast.7) | data formatting | bytes 294912
  92.4 0.0 copy-start
  92.4 2.1 %copy.13 = bf16[1,144,3072]{2,1,0:T(8,128)(2,1)} copy(bf16[1,144,3072]{2,1,0:T(8,128)(2,1)} %bitcast.5) | data formatting | bytes 1769472
  94.6 0.0 copy-done
  94.6 0.6 copy.14
Async XLA Ops:
  92.4 2.1 %copy-start = (f32[8,64]{1,0:T(8,128)S(1)}, f32[8,64]{1,0:T(8,128)}, u32[]{:S(2)}) copy-start(f32[8,64]{1,0:T(8,128)} %get-tuple-element.8) | copy-start | bytes 6148

commit v4 on v3

--- a/solution.py
+++ b/solution.py
@@ -300,7 +300,7 @@
     def back_start(i):
         grp_start(rs[i], rr[i], r_ssem.at[i], r_rsem.at[i])
 
-    back(0, jnp.concatenate([normed[:, : 3 * DH], normed[:, 4 * DH :]], axis=1), normed[:, head(3)])
+    back(0, normed[:, : 3 * DH], normed[:, head(3)])
 
     back_start(0)
 
@@ -343,13 +343,9 @@
         ds = (mm_nt(datt[:, head(h)], vs[h]) * f_scr[h]).astype(BF)
         return [mm(ds, ks[h]) * scale, mm_tn(ds, qs[h]) * scale]
 
-    def back_heads(i):
-        a = 3 * (i - 1)
-        natural = dqk(a) + dqk(a + 1) + dqk(a + 2) + [dv(a)]
-        back(i, jnp.concatenate(natural, axis=1), jnp.concatenate([dv(a + 1), dv(a + 2)], axis=1))
-        back_start(i)
-
-    back_heads(1)
+    natural = [normed[:, 4 * DH :]] + dqk(0) + dqk(1) + dqk(2) + [dv(0)]
+    back(1, jnp.concatenate(natural, axis=1), jnp.concatenate([dv(1), dv(2), dv(3)], axis=1))
+    back_start(1)
     own = mm(ogt_ref[core], zo)
     d1.wait_recv()
     d2s[...] = (own + d1r[...].astype(F32)).astype(BF).reshape(NY, 32, HD)
@@ -368,7 +364,7 @@
 
     lax.fori_loop(1, NY, d2_start, 0)
     d2r[y] = d2s[y]
-    back_heads(2)
+    back(2, jnp.concatenate(dqk(3) + dqk(4) + dqk(5), axis=1), jnp.concatenate([dv(4), dv(5)], axis=1))
 
     def chunk_home(i):
         grp_wait_recv(rs[i], rr[i], r_ssem.at[i], r_rsem.at[i])
@@ -400,6 +396,7 @@
         return c
 
     lax.fori_loop(1, NX, d3_start, 0)
+    back_start(2)
     d3r[gx] = d3s[gx]
 
     def d3_wait(k, c):
@@ -430,25 +427,28 @@
     lax.fori_loop(1, NG, d4_start, 0)
     d4r[place] = d4s[place]
 
-    n_part, chunk = chunk_home(0)
+    n_part, chunk0 = chunk_home(0)
+    part, chunk = chunk_home(1)
     n_home = jnp.concatenate(
-        [n_part[:, : 3 * DH], fold_out(home_fold, chunk, 1), n_part[:, 3 * DH :]], axis=1
+        [n_part, fold_out(home_fold, chunk0, 1), part[:, : 2 * DH]], axis=1
     )
     z = (n_home * gate).astype(BF)
     pg_ref[:, :HD] = (branch * n_home).astype(BF)
     bo_ref[...] = mm(z, w_ref[...]).astype(BF)
-
-    for i in (1, 2):
-        a = 3 * (i - 1)
-        part, chunk = chunk_home(i)
-        part = part.astype(BF)
-        for h in range(3):
-            lo = 2 * HD + (a + h) * DH
-            pg_ref[:, lo : lo + DH] = part[:, head(2 * h)]
-            pg_ref[:, lo + HD : lo + HD + DH] = part[:, head(2 * h + 1)]
-        lo = HD + a * DH
-        pg_ref[:, lo : lo + DH] = part[:, head(6)]
-        pg_ref[:, lo + DH : lo + 3 * DH] = fold_out(home_fold, chunk, 2).astype(BF)
+    part = part.astype(BF)
+    for h in range(3):
+        lo = 2 * HD + h * DH
+        pg_ref[:, lo : lo + DH] = part[:, head(2 * h + 2)]
+        pg_ref[:, lo + HD : lo + HD + DH] = part[:, head(2 * h + 3)]
+    pg_ref[:, HD : HD + DH] = part[:, head(8)]
+    pg_ref[:, HD + DH : HD + 4 * DH] = fold_out(home_fold, chunk, 3).astype(BF)
+    part, chunk = chunk_home(2)
+    part = part.astype(BF)
+    for h in range(3):
+        lo = 2 * HD + (h + 3) * DH
+        pg_ref[:, lo : lo + DH] = part[:, head(2 * h)]
+        pg_ref[:, lo + HD : lo + HD + DH] = part[:, head(2 * h + 1)]
+    pg_ref[:, HD + 4 * DH : half] = fold_out(home_fold, chunk, 2).astype(BF)
 
     def d4_wait(k, c):
         d4(k, True).wait_recv()
@@ -505,7 +505,7 @@
             pltpu.VMEM((ROWS, 512), BF),
             pltpu.VMEM((HD, 512), BF),
             dma((4,)),
-            *[pltpu.VMEM((NG, PR, w), BF) for w in (768, 768, 384, 768) * 2 + (640, 896, 896) * 2],
+            *[pltpu.VMEM((NG, PR, w), BF) for w in (768, 768, 384, 768) * 2 + (384, 1152, 768) * 2],
             pltpu.VMEM((NG, 1, DH), F32),
             pltpu.VMEM((NG, 1, DH), F32),
             pltpu.VMEM((HEADS, PROWS, PROWS), BF),

time: 95.4 us -> 92.4 us (0.969)
  the two profiles are of different devices: /device:TPU:32 before, /device:TPU:1 now
where the time goes in v4:
time: 92.4 us; the launch traced here: 92.1 us
  Pallas kernels  87.2 us (94%)
  local copies, waits for them, and re-layouts  4.31 us (5%)
    pallas_call x1, Pallas kernels, per_device(): pl.pallas_call(kernel, out_shape=(jax.ShapeDtypeStruct((ROWS, 512), BF),...  87.2 us
    unnamed x5, local copies, waits for them, and re-layouts  4.31 us

profile of v4, /device:TPU:1, one launch (start us, length us, event | category | flops | bytes accessed | tf_op | source)
XLA Modules:
  0.0 92.1 jit_solution(8724320952139740781)
XLA Ops:
  0.6 87.2 %shard_map.85 = (bf16[144,512]{1,0:T(8,128)(2,1)}, bf16[144,3072]{1,0:T(8,128)(2,1)}, f32[8,64]{1,0:T(8,128)}) custom-call(s32[1,12]{1,0:T(1,128)} %own_s.1, s32[1,12]{1,0:T(1,128)} %slot_s.1, s32[1,12]{1,0:T(1,128)} %len_s.1, bf16[144,3072]{1,0:T(8,128)(2,1)} %bitcast.6, bf16[144,512]{1,0:T(8,128)(2,1)} %bitcast.8, bf16[768,512]{1,0:T(8,128)(2,1)} %w_hbm.1), custom_call_target="tpu_custom_call" | custom-call | tf_op jit(solution)/shard_map/pallas_call | solution.py:494
  87.8 1.6 %copy.12 = bf16[1,144,512]{2,1,0:T(8,128)(2,1)} copy(bf16[1,144,512]{2,1,0:T(8,128)(2,1)} %bitcast.7) | data formatting | bytes 294912
  89.4 0.0 copy-start
  89.4 2.1 %copy.13 = bf16[1,144,3072]{2,1,0:T(8,128)(2,1)} copy(bf16[1,144,3072]{2,1,0:T(8,128)(2,1)} %bitcast.5) | data formatting | bytes 1769472
  91.5 0.0 copy-done
  91.6 0.6 copy.14
Async XLA Ops:
  89.4 2.1 %copy-start = (f32[8,64]{1,0:T(8,128)S(1)}, f32[8,64]{1,0:T(8,128)}, u32[]{:S(2)}) copy-start(f32[8,64]{1,0:T(8,128)} %get-tuple-element.8) | copy-start | bytes 6148

commit v5 on v4

--- a/solution.py
+++ b/solution.py
@@ -310,6 +310,24 @@
     )
     og_o = jnp.concatenate([c3[:, 4 * DH :], fold_out(unfold, c3, 2).astype(BF)], axis=1)
 
+    gr = mm_nt(og_o, w_ref[...]).astype(BF).astype(F32) * gate_o
+    datt = rstd * (
+        gr - jnp.mean(gr, axis=1, keepdims=True)
+        - normed * jnp.mean(gr * normed, axis=1, keepdims=True)
+    )
+    datt = jnp.where(valid > 0.5, datt, 0.0).astype(BF)
+
+    def dv(h):
+        return mm_tn(p_scr[h], datt[:, head(h)])
+
+    def dqk(h):
+        ds = (mm_nt(datt[:, head(h)], vs[h]) * f_scr[h]).astype(BF)
+        return [mm(ds, ks[h]) * scale, mm_tn(ds, qs[h]) * scale]
+
+    natural = [normed[:, 4 * DH :]] + dqk(0) + dqk(1) + dqk(2) + [dv(0)]
+    back(1, jnp.concatenate(natural, axis=1), jnp.concatenate([dv(1), dv(2), dv(3)], axis=1))
+    back_start(1)
+
     ogt = jnp.transpose(og_o.astype(F32))
     for cc in range(NC):
         ogt_ref[cc] = jnp.concatenate(
@@ -328,24 +346,6 @@
         device_id=(g, other), device_id_type=MESH,
     )
     d1.start()
-
-    gr = mm_nt(og_o, w_ref[...]).astype(BF).astype(F32) * gate_o
-    datt = rstd * (
-        gr - jnp.mean(gr, axis=1, keepdims=True)
-        - normed * jnp.mean(gr * normed, axis=1, keepdims=True)
-    )
-    datt = jnp.where(valid > 0.5, datt, 0.0).astype(BF)
-
-    def dv(h):
-        return mm_tn(p_scr[h], datt[:, head(h)])
-
-    def dqk(h):
-        ds = (mm_nt(datt[:, head(h)], vs[h]) * f_scr[h]).astype(BF)
-        return [mm(ds, ks[h]) * scale, mm_tn(ds, qs[h]) * scale]
-
-    natural = [normed[:, 4 * DH :]] + dqk(0) + dqk(1) + dqk(2) + [dv(0)]
-    back(1, jnp.concatenate(natural, axis=1), jnp.concatenate([dv(1), dv(2), dv(3)], axis=1))
-    back_start(1)
     own = mm(ogt_ref[core], zo)
     d1.wait_recv()
     d2s[...] = (own + d1r[...].astype(F32)).astype(BF).reshape(NY, 32, HD)

time: 92.4 us -> 94.1 us (1.018); the launches traced: 92.1 us -> 92.6 us
  no operation moved by 1% of the time
where the time goes in v5:
time: 94.1 us; the launch traced here: 92.6 us
  Pallas kernels  87.6 us (93%)
  local copies, waits for them, and re-layouts  4.31 us (5%)
    pallas_call x1, Pallas kernels, per_device(): pl.pallas_call(kernel, out_shape=(jax.ShapeDtypeStruct((ROWS, 512), BF),...  87.6 us
    unnamed x5, local copies, waits for them, and re-layouts  4.31 us

profile of v5, /device:TPU:1, one launch (start us, length us, event | category | flops | bytes accessed | tf_op | source)
XLA Modules:
  0.0 92.6 jit_solution(9571809236655303025)
XLA Ops:
  0.6 87.6 %shard_map.85 = (bf16[144,512]{1,0:T(8,128)(2,1)}, bf16[144,3072]{1,0:T(8,128)(2,1)}, f32[8,64]{1,0:T(8,128)}) custom-call(s32[1,12]{1,0:T(1,128)} %own_s.1, s32[1,12]{1,0:T(1,128)} %slot_s.1, s32[1,12]{1,0:T(1,128)} %len_s.1, bf16[144,3072]{1,0:T(8,128)(2,1)} %bitcast.6, bf16[144,512]{1,0:T(8,128)(2,1)} %bitcast.8, bf16[768,512]{1,0:T(8,128)(2,1)} %w_hbm.1), custom_call_target="tpu_custom_call" | custom-call | tf_op jit(solution)/shard_map/pallas_call | solution.py:494
  88.3 1.6 %copy.12 = bf16[1,144,512]{2,1,0:T(8,128)(2,1)} copy(bf16[1,144,512]{2,1,0:T(8,128)(2,1)} %bitcast.7) | data formatting | bytes 294912
  89.8 0.0 copy-start
  89.8 2.1 %copy.13 = bf16[1,144,3072]{2,1,0:T(8,128)(2,1)} copy(bf16[1,144,3072]{2,1,0:T(8,128)(2,1)} %bitcast.5) | data formatting | bytes 1769472
  92.0 0.0 copy-done
  92.0 0.6 copy.14
Async XLA Ops:
  89.8 2.1 %copy-start = (f32[8,64]{1,0:T(8,128)S(1)}, f32[8,64]{1,0:T(8,128)}, u32[]{:S(2)}) copy-start(f32[8,64]{1,0:T(8,128)} %get-tuple-element.8) | copy-start | bytes 6148
